TPU v7x, 32 devices: a whole 2x2x4 slice. The times are simulated.
32 devices in a mesh: clip: 4 (over x, core), frame: 8 (over z, y).
Axes of the slice: x: 2, y: 2, z: 4, core: 2. Of those that a mesh axis runs over, the one named last changes fastest.
Arguments:
- stream: bfloat16 [64, 256, 768], P(('clip', 'frame')), may hold values from -24 to 24
- out_grad: bfloat16 [64, 256, 768], P(('clip', 'frame')), may hold values from -6 to 6
- token_mask: int32 [64, 256], P(('clip', 'frame')), may hold values from 0 to 1, as said below
- ln1_gain: float32 [768], replicated, may hold values from 0.25 to 1.75
- ln1_bias: float32 [768], replicated, may hold values from -3 to 3
- w_qkv: bfloat16 [768, 2304], replicated, may hold values from -0.3125 to 0.3125
- b_qv: float32 [1536], replicated, may hold values from -4 to 4
- w_out: bfloat16 [768, 768], replicated, may hold values from -0.4375 to 0.4375
- b_out: float32 [768], replicated, may hold values from -3 to 3
- ln2_gain: float32 [768], replicated, may hold values from 0.25 to 1.75
- ln2_bias: float32 [768], replicated, may hold values from -3 to 3
- w_up: bfloat16 [768, 3072], replicated, may hold values from -0.21875 to 0.21875
- b_up: float32 [3072], replicated, may hold values from -4 to 4
- w_down: bfloat16 [3072, 768], replicated, may hold values from -0.109375 to 0.109375
- b_down: float32 [768], replicated, may hold values from -3 to 3
Outputs:
- output: bfloat16 [64, 256, 768], P(('clip', 'frame'))
- input_grad: bfloat16 [64, 256, 768], P(('clip', 'frame'))
- grad_ln1_gain: float32 [768], P('frame')
- grad_ln1_bias: float32 [768], P('frame')
- grad_w_qkv: float32 [768, 2304], P('frame')
- grad_b_qv: float32 [1536], P('frame')
- grad_w_out: float32 [768, 768], P('frame')
- grad_b_out: float32 [768], P('frame')
- grad_ln2_gain: float32 [768], P('frame')
- grad_ln2_bias: float32 [768], P('frame')
- grad_w_up: float32 [768, 3072], P('frame')
- grad_b_up: float32 [3072], P('frame')
- grad_w_down: float32 [3072, 768], P('frame')
- grad_b_down: float32 [768], P('frame')
- statistics: float32 [5], replicated
Inputs may be any that keep to these rules, and one draw needn't show every extreme that they name: `token_mask`: each clip draws its own chance of a masked token, from one half to one.
All inputs are finite; a program needn't handle non-finite values.
Results may differ from a plain program's by a relative error of at most 0.015.
Values may be sent and summed in bfloat16 or wider, within the bound.
A program may use at most 192 MiB of HBM per device.

v0:
```python
import math

import jax
import jax.numpy as jnp
from jax import lax
from jax.sharding import PartitionSpec as P

HEADS = 12
FRAMES = 16
TUBES = 16


EPS = 1e-05


def layer_norm(inputs, norm_gain, norm_shift):
    center = jnp.mean(inputs, axis=-1, keepdims=True)
    shifted = inputs - center
    spread = jnp.mean(shifted * shifted, axis=-1, keepdims=True)
    inverse = lax.rsqrt(spread + EPS)
    unit = shifted * inverse
    return (unit * norm_gain + norm_shift, unit, inverse)


def norm_backward(upstream, unit, inverse, norm_gain):
    scaled = upstream * norm_gain
    first = jnp.mean(scaled, axis=-1, keepdims=True)
    second = jnp.mean(scaled * unit, axis=-1, keepdims=True)
    return inverse * (scaled - first - unit * second)


def gelu_slope(hidden_state):
    cumulative = 0.5 * (1.0 + lax.erf(hidden_state * (1.0 / math.sqrt(2.0))))
    density = jnp.exp(-0.5 * hidden_state * hidden_state) * (1.0 / math.sqrt(2.0 * math.pi))
    return cumulative + hidden_state * density


def on_device(
    stream,
    out_grad,
    token_mask,
    ln1_gain,
    ln1_bias,
    w_qkv,
    b_qv,
    w_out,
    b_out,
    ln2_gain,
    ln2_bias,
    w_up,
    b_up,
    w_down,
    b_down,
):
    frame_count = lax.axis_size("frame")
    clip_count = lax.axis_size("clip")
    device_count = clip_count * frame_count
    frame_split = min(FRAMES, frame_count)
    clip_split = frame_count // frame_split
    frames_dev = FRAMES // frame_split
    tubes_dev = TUBES // frame_split
    row_count, spatial, width = stream.shape
    clips_dev = row_count // frames_dev
    clip_sets = clips_dev // clip_split
    tube_pos = spatial // TUBES
    length = FRAMES * tube_pos
    head_dim = width // HEADS
    scale = 1.0 / math.sqrt(head_dim)

    def leaving(tensor):
        return tensor.reshape(frames_dev, clip_sets, frame_count, tubes_dev * tube_pos, width)

    def arranged(tensor):
        tensor = tensor.reshape(clip_split, FRAMES, clip_sets, tubes_dev, tube_pos, width)
        tensor = jnp.transpose(tensor, (0, 2, 3, 1, 4, 5))
        return tensor.reshape(-1, width)

    def restored(tensor):
        tensor = tensor.reshape(clip_split, clip_sets, tubes_dev, FRAMES, tube_pos, width)
        tensor = jnp.transpose(tensor, (0, 3, 1, 2, 4, 5))
        return tensor.reshape(frame_count * frames_dev, clip_sets, 1, tubes_dev * tube_pos, width)

    masked = jnp.where(token_mask[:, :, None] == 1, out_grad, jnp.zeros((), jnp.bfloat16))
    arrived = (
        lax.all_to_all(leaving(stream), "frame", split_axis=2, concat_axis=0, tiled=True),
        lax.all_to_all(leaving(masked), "frame", split_axis=2, concat_axis=0, tiled=True),
    )
    inputs = arranged(arrived[0]).astype(jnp.float32)
    grad_y = arranged(arrived[1])
    seq_count = inputs.shape[0] // length

    def split_heads(tensor):
        return tensor.reshape(seq_count, length, HEADS, head_dim)

    def attention_scores(queries, key_part):
        return (
            jnp.einsum("slhe,smhe->shlm", queries, key_part, preferred_element_type=jnp.float32)
            * scale
        )

    first_normed_input, unit_one, inverse_one = layer_norm(inputs, ln1_gain, ln1_bias)
    first_normed_input = first_normed_input.astype(jnp.bfloat16)
    third_bias_term = jnp.concatenate(
        [b_qv[:width], jnp.zeros((width,), jnp.float32), b_qv[width:]]
    )
    query_key_value = (
        jnp.dot(first_normed_input, w_qkv, preferred_element_type=jnp.float32) + third_bias_term
    ).astype(jnp.bfloat16)
    queries = split_heads(query_key_value[:, :width])
    key_part = split_heads(query_key_value[:, width : 2 * width])
    values = split_heads(query_key_value[:, 2 * width :])
    scores = attention_scores(queries, key_part)
    largest = jnp.max(scores, axis=-1, keepdims=True)
    logsum = largest + jnp.log(jnp.sum(jnp.exp(scores - largest), axis=-1, keepdims=True))
    attend_low = jnp.exp(scores - logsum).astype(jnp.bfloat16)
    mixed_heads = jnp.einsum(
        "shlm,smhe->slhe", attend_low, values, preferred_element_type=jnp.float32
    )
    mixed_heads = mixed_heads.reshape(-1, width).astype(jnp.bfloat16)
    attention_branch = jnp.dot(mixed_heads, w_out, preferred_element_type=jnp.float32) + b_out
    middle = inputs + attention_branch
    second_normed_input, unit_two, inverse_two = layer_norm(middle, ln2_gain, ln2_bias)
    second_normed_input = second_normed_input.astype(jnp.bfloat16)
    hidden_state = jnp.dot(second_normed_input, w_up, preferred_element_type=jnp.float32) + b_up
    activated_hidden = jax.nn.gelu(hidden_state, approximate=False).astype(jnp.bfloat16)
    feedforward_branch = (
        jnp.dot(activated_hidden, w_down, preferred_element_type=jnp.float32) + b_down
    )
    result = middle + feedforward_branch
    squares = jnp.stack(
        [
            jnp.sum(inputs * inputs),
            jnp.sum(middle * middle),
            jnp.sum(result * result),
            jnp.sum(attention_branch * attention_branch),
            jnp.sum(feedforward_branch * feedforward_branch),
        ]
    )
    totals = lax.psum(squares, ("clip", "frame"))
    statistics = jnp.sqrt(totals / (row_count * spatial * width * device_count))
    grad_w_down = jnp.einsum(
        "tf,td->fd", activated_hidden, grad_y, preferred_element_type=jnp.float32
    )
    grad_b_down = jnp.sum(grad_y.astype(jnp.float32), axis=0)
    d_active = jnp.einsum("td,fd->tf", grad_y, w_down, preferred_element_type=jnp.float32)
    d_hidden = (d_active * gelu_slope(hidden_state)).astype(jnp.bfloat16)
    grad_w_up = jnp.einsum(
        "td,tf->df", second_normed_input, d_hidden, preferred_element_type=jnp.float32
    )
    grad_b_up = jnp.sum(d_hidden.astype(jnp.float32), axis=0)
    d_two = jnp.einsum("tf,df->td", d_hidden, w_up, preferred_element_type=jnp.float32)
    grad_ln2_gain = jnp.sum(d_two * unit_two, axis=0)
    grad_ln2_bias = jnp.sum(d_two, axis=0)
    d_middle = grad_y.astype(jnp.float32) + norm_backward(d_two, unit_two, inverse_two, ln2_gain)
    d_branch = d_middle.astype(jnp.bfloat16)
    grad_w_out = jnp.einsum("td,te->de", mixed_heads, d_branch, preferred_element_type=jnp.float32)
    grad_b_out = jnp.sum(d_branch.astype(jnp.float32), axis=0)
    d_mixed = jnp.einsum("te,de->td", d_branch, w_out, preferred_element_type=jnp.float32)
    d_mixed = split_heads(d_mixed.astype(jnp.bfloat16))
    again = attention_scores(queries, key_part)
    attend = jnp.exp(again - logsum)
    attend_again = attend.astype(jnp.bfloat16)
    d_attend = jnp.einsum("slhe,smhe->shlm", d_mixed, values, preferred_element_type=jnp.float32)
    d_values = jnp.einsum(
        "shlm,slhe->smhe", attend_again, d_mixed, preferred_element_type=jnp.float32
    )
    centre_term = jnp.sum(attend * d_attend, axis=-1, keepdims=True)
    d_scores = (attend * (d_attend - centre_term)).astype(jnp.bfloat16)
    d_queries = (
        jnp.einsum("shlm,smhe->slhe", d_scores, key_part, preferred_element_type=jnp.float32)
        * scale
    )
    d_keys = (
        jnp.einsum("shlm,slhe->smhe", d_scores, queries, preferred_element_type=jnp.float32) * scale
    )
    d_qkv = jnp.concatenate(
        [d_queries.reshape(-1, width), d_keys.reshape(-1, width), d_values.reshape(-1, width)],
        axis=1,
    ).astype(jnp.bfloat16)
    grad_w_qkv = jnp.einsum(
        "td,te->de", first_normed_input, d_qkv, preferred_element_type=jnp.float32
    )
    bias_sums = jnp.sum(d_qkv.astype(jnp.float32), axis=0)
    grad_b_qv = jnp.concatenate([bias_sums[:width], bias_sums[2 * width :]])
    d_one = jnp.einsum("te,de->td", d_qkv, w_qkv, preferred_element_type=jnp.float32)
    grad_ln1_gain = jnp.sum(d_one * unit_one, axis=0)
    grad_ln1_bias = jnp.sum(d_one, axis=0)
    d_inputs = d_middle + norm_backward(d_one, unit_one, inverse_one, ln1_gain)
    departed = (
        lax.all_to_all(
            restored(result.astype(jnp.bfloat16)), "frame", split_axis=0, concat_axis=2, tiled=True
        ),
        lax.all_to_all(
            restored(d_inputs.astype(jnp.bfloat16)),
            "frame",
            split_axis=0,
            concat_axis=2,
            tiled=True,
        ),
    )
    output = departed[0].reshape(row_count, spatial, width)
    input_grad = departed[1].reshape(row_count, spatial, width)
    gradients = [
        grad_ln1_gain,
        grad_ln1_bias,
        grad_w_qkv,
        grad_b_qv,
        grad_w_out,
        grad_b_out,
        grad_ln2_gain,
        grad_ln2_bias,
        grad_w_up,
        grad_b_up,
        grad_w_down,
        grad_b_down,
    ]
    grouped = jnp.concatenate([item.reshape(frame_count, -1) for item in gradients], axis=1)
    extent_all = grouped.shape[1]
    padding = -extent_all % clip_count
    grouped = jnp.concatenate([grouped, jnp.zeros((frame_count, padding), jnp.float32)], axis=1)
    own_rows = lax.psum_scatter(
        grouped.astype(jnp.bfloat16), "frame", scatter_dimension=0, tiled=True
    ).astype(jnp.float32)
    summed = lax.psum(own_rows, "clip").reshape(-1)
    finished = []
    offset = 0
    for item in gradients:
        extent = item.size // frame_count
        local_shape = (item.shape[0] // frame_count,) + item.shape[1:]
        finished.append(summed[offset : offset + extent].reshape(local_shape))
        offset = offset + extent
    return (
        output,
        input_grad,
        finished[0],
        finished[1],
        finished[2],
        finished[3],
        finished[4],
        finished[5],
        finished[6],
        finished[7],
        finished[8],
        finished[9],
        finished[10],
        finished[11],
        statistics,
    )


def solution(mesh):
    in_specs = (
        P(("clip", "frame"), None, None),
        P(("clip", "frame"), None, None),
        P(("clip", "frame"), None),
        P(),
        P(),
        P(),
        P(),
        P(),
        P(),
        P(),
        P(),
        P(),
        P(),
        P(),
        P(),
    )
    out_specs = (
        P(("clip", "frame"), None, None),
        P(("clip", "frame"), None, None),
        P("frame"),
        P("frame"),
        P("frame", None),
        P("frame"),
        P("frame", None),
        P("frame"),
        P("frame"),
        P("frame"),
        P("frame", None),
        P("frame"),
        P("frame", None),
        P("frame"),
        P(),
    )
    return jax.shard_map(
        on_device, mesh=mesh, in_specs=in_specs, out_specs=out_specs, check_vma=False
    )
```

profile of v0, /device:TPU:1, one launch (start us, length us, event | category | flops | bytes accessed | tf_op | source)
XLA Modules:
  0.0 885.4 jit_solution(17268720271331708220)
XLA Ops:
  7.2 2.2 copy.128
  9.4 6.4 all-to-all-start
  18.7 16.3 %all-to-all-done = bf16[2,1,8,32,768]{4,3,0,1,2:T(8,128)(2,1)} async-done(((bf16[2,1,8,32,768]{4,3,0,1,2:T(8,128)(2,1)}), bf16[2,1,8,32,768]{4,3,0,1,2:T(8,128)(2,1)}, u32[]{:S(2)}, u32[]{:S(2)}) %all-to-all-start) | async-done | bytes 786464 | tf_op jit(solution)/shard_map/all_to_all | solution.py:85
  35.0 4.9 all-to-all-start.2
  40.5 2.4 bitcast_convert_fusion
  43.0 2.2 reduce_sum.207
  47.1 2.7 copy.130
  49.8 8.9 %all-to-all-done.2 = bf16[2,1,8,32,768]{4,3,0,1,2:T(8,128)(2,1)} async-done(((bf16[2,1,8,32,768]{4,3,0,1,2:T(8,128)(2,1)}), bf16[2,1,8,32,768]{4,3,0,1,2:T(8,128)(2,1)}, u32[]{:S(2)}, u32[]{:S(2)}) %all-to-all-start.2) | async-done | bytes 786464 | tf_op jit(solution)/shard_map/all_to_all | solution.py:86
  58.7 2.1 copy.146
  60.9 2.5 multiply_reduce_fusion.6
  64.0 1.7 add_convert_fusion.2
  65.8 2.7 fusion.16
  70.0 2.3 copy.135
  72.3 2.9 reshape.274
  75.2 2.3 copy.136
  77.5 2.9 reshape.275
  80.4 2.3 copy.134
  82.7 3.1 reshape.273
  85.8 2.4 multiply_reduce_fusion.1
  92.7 1.6 fusion.43
  94.8 16.0 %fusion.2 = (bf16[512,3072]{1,0:T(8,128)(2,1)S(1)}, f32[512,3072]{1,0:T(8,128)S(1)}) fusion(f32[3072]{0:T(1024)S(1)} %copy-done.26, bf16[768,3072]{1,0:T(8,128)(2,1)S(1)} %bitcast.159, f32[512,768]{1,0:T(8,128)S(1)} %get-tuple-element.36, f32[768]{0:T(1024)S(1)} %copy-done.28, f32[768]{0:T(1024)S(1)} %copy-done.23, f32[512]{0:T(512)S(1)} %add_rsqrt_fusion, ...), kind=kOutput, calls=%fused_computation.4 | convolution fusion | flops 2521694208 | bytes 15751168 | tf_op jit(solution)/shard_map/dot_general | solution.py:124
  110.8 5.7 fusion.47
  116.5 2.7 fusion.48
  119.1 4.8 convolution_convert_fusion.1
  124.0 4.8 multiply_reduce_fusion.2
  130.1 1.8 convolution_convert_fusion.3
  131.9 1.7 convolution_convert_fusion.5
  133.6 4.4 convolution_convert_fusion
  137.9 2.3 copy.147
  140.3 3.1 reshape.282
  143.4 4.3 fusion.22
  147.8 7.2 multiply_reduce_fusion
  154.9 4.6 multiply_convert_fusion
  164.7 4.2 multiply_reduce_fusion.8
  168.8 4.0 convolution_convert_fusion.2
  172.9 2.6 reduce.4
  179.5 6.6 reshape.296
  188.8 2.8 reshape.292
  191.6 6.6 reshape.298
  204.9 5.4 reshape.291
  214.4 19.6 %dynamic-update-slice.2 = bf16[8,885888]{1,0:T(8,128)(2,1)} dynamic-update-slice(bf16[8,885888]{1,0:T(8,128)(2,1)} %dynamic-update-slice.1, bf16[8,221184]{1,0:T(8,128)(2,1)} %reshape.291, s32[]{} %constant.110, s32[]{} %constant.112) | dynamic-update-slice | bytes 7077892
  234.0 1.4 dynamic-update-slice.3
  235.4 2.4 constant_dynamic-update-slice_fusion.3
  242.0 25.6 %dynamic-update-slice.8 = bf16[8,885888]{1,0:T(8,128)(2,1)} dynamic-update-slice(bf16[8,885888]{1,0:T(8,128)(2,1)} %dynamic-update-slice.7, bf16[8,294912]{1,0:T(8,128)(2,1)} %reshape.296, s32[]{} %constant.110, s32[]{} %constant.119) | dynamic-update-slice | bytes 9437188
  267.6 1.5 dynamic-update-slice.9
  269.1 25.3 %dynamic-update-slice.10 = bf16[8,885888]{1,0:T(8,128)(2,1)} dynamic-update-slice(bf16[8,885888]{1,0:T(8,128)(2,1)} %dynamic-update-slice.9, bf16[8,294912]{1,0:T(8,128)(2,1)} %reshape.298, s32[]{} %constant.110, s32[]{} %constant.121) | dynamic-update-slice | bytes 9437188
  297.0 2.1 copy.142
  299.1 5.1 all-to-all-start.1
  304.3 448.0 %all-reduce.6.cloned.1.call-done = bf16[8,885888]{1,0:T(8,128)(2,1)} async-done(((bf16[8,885888]{1,0:T(8,128)(2,1)}), bf16[8,885888]{1,0:T(8,128)(2,1)}) %all-reduce.6.cloned.1.call-update) | async-done | bytes 14174224
  752.3 8.5 dynamic-slice_convert_fusion
  761.5 2.9 add_convert_fusion
  765.3 4.5 all-to-all-start.3
  769.8 3.3 stack.23
  773.1 42.1 %psum.15 = f32[5]{0:T(128)S(1)} all-reduce(f32[5]{0:T(128)S(1)} %stack.23), channel_id=1, replica_groups=mesh['clip'=4,'frame'=8] {'clip','frame'}, use_global_device_ids=true, to_apply=%region_26.27 | all-reduce | flops 5 | bytes 40 | tf_op jit(solution)/shard_map/psum | solution.py:139
  815.7 2.1 copy.144
  817.8 2.1 copy.161
  819.9 16.8 %all-reduce.4.cloned.1.call-done = f32[1,885888]{1,0:T(1,128)} async-done(((f32[1,885888]{1,0:T(1,128)}), f32[1,885888]{1,0:T(1,128)}) %all-reduce.4.cloned.1.call-update) | async-done | bytes 3543568 | tf_op jit(solution)/shard_map/psum | solution.py:224
  836.7 2.4 slice_reduce_fusion.3
  839.1 1.7 reshape.301
  840.8 15.0 %slice_reduce_fusion = (f32[294912]{0:T(1024)}, f32[294912]{0:T(1024)}) fusion(f32[1,885888]{1,0:T(1,128)} %all-reduce.4.cloned.1.call-done), kind=kLoop, calls=%fused_computation.71 | loop fusion | bytes 4718592 | tf_op jit(solution)/shard_map/slice | solution.py:230
  855.9 2.4 reshape.303
  858.3 11.2 %slice_reduce_fusion.2 = f32[221184]{0:T(1024)} fusion(f32[1,885888]{1,0:T(1,128)} %all-reduce.4.cloned.1.call-done), kind=kLoop, calls=%fused_computation.73 | loop fusion | bytes 1769472 | tf_op jit(solution)/shard_map/slice | solution.py:230
  869.4 2.2 reshape.300
  871.7 2.4 reshape.302
  (143 shorter events, 49.1 us)
Async XLA Ops:
  7.2 58.6 %copy-start = (bf16[768,2304]{1,0:T(8,128)(2,1)S(1)}, bf16[768,2304]{1,0:T(8,128)(2,1)}, u32[]{:S(2)}) copy-start(bf16[768,2304]{1,0:T(8,128)(2,1)} %param.20) | copy-start | bytes 10616836
  7.2 32.7 %copy-start.21 = (f32[1536]{0:T(1024)S(1)}, f32[1536]{0:T(1024)}, u32[]{:S(2)}) copy-start(f32[1536]{0:T(1024)} %param.21) | copy-start | bytes 18436
  9.4 25.5 %all-to-all-start = ((bf16[2,1,8,32,768]{4,3,0,1,2:T(8,128)(2,1)}), bf16[2,1,8,32,768]{4,3,0,1,2:T(8,128)(2,1)}, u32[]{:S(2)}, u32[]{:S(2)}) async-start(bf16[2,1,8,32,768]{4,3,0,1,2:T(8,128)(2,1)} %copy.128), calls=%async_computation | async-start | bytes 1572864 | tf_op jit(solution)/shard_map/all_to_all | solution.py:85
  35.0 23.8 %all-to-all-start.2 = ((bf16[2,1,8,32,768]{4,3,0,1,2:T(8,128)(2,1)}), bf16[2,1,8,32,768]{4,3,0,1,2:T(8,128)(2,1)}, u32[]{:S(2)}, u32[]{:S(2)}) async-start(bf16[2,1,8,32,768]{4,3,0,1,2:T(8,128)(2,1)} %copy.145), calls=%async_computation.2 | async-start | bytes 1572864 | tf_op jit(solution)/shard_map/all_to_all | solution.py:86
  39.8 712.4 %all-reduce.6.cloned.1.call-start = ((), (), s32[]{:S(2)}) async-start(), calls=%async_computation.5 | async-start | bytes 28348416
  47.1 13.7 %copy-start.16 = (f32[2,16,16]{2,0,1:T(2,128)S(1)}, f32[2,16,16]{2,0,1:T(2,128)}, u32[]{:S(2)}) copy-start(f32[2,16,16]{2,0,1:T(2,128)} %copy.132) | copy-start | bytes 6148
  65.8 2.8 copy-start.14
  88.2 3.5 copy-start.1
  88.2 2.2 copy-start.7
  89.3 1.1 copy-start.12
  90.4 2.3 copy-start.2
  90.4 2.3 copy-start.25
  90.4 2.3 copy-start.27
  90.4 4.2 slice-start.2
  91.6 3.0 slice-start.3
  92.7 2.0 copy-start.23
  92.7 2.0 copy-start.26
  92.7 2.0 copy-start.28
  92.7 18.0 %slice-start.4 = ((s8[4718592]{0:T(1024)(128)(4,1)}), s8[4194304]{0:T(1024)(128)(4,1)S(1)}, s32[]{:S(2)}) async-start(s8[4718592]{0:T(1024)(128)(4,1)} %bitcast.160), calls=%async_computation.10 | async-start | bytes 8388608
  94.7 16.0 %copy-start.11 = (bf16[1,1,2,16,16,768]{5,4,3,2,1,0:T(8,128)(2,1)S(1)}, bf16[1,1,2,16,16,768]{5,4,3,2,1,0:T(8,128)(2,1)}, u32[]{:S(2)}) copy-start(bf16[1,1,2,16,16,768]{5,4,3,2,1,0:T(8,128)(2,1)} %copy.146) | copy-start | bytes 2359300
  94.7 16.0 %slice-start.5 = ((s8[4718592]{0:T(1024)(128)(4,1)}), s8[524288]{0:T(1024)(128)(4,1)S(1)}, s32[]{:S(2)}) async-start(s8[4718592]{0:T(1024)(128)(4,1)} %bitcast.160), calls=%async_computation.11 | async-start | bytes 1048576
  119.1 4.9 copy-start.29
  130.1 1.8 copy-start.4
  143.3 4.4 copy-start.8
  143.3 4.4 copy-start.9
  143.4 4.4 copy-start.13
  143.4 11.6 %slice-start = ((s8[6291456]{0:T(1024)(128)(4,1)}), s8[4194304]{0:T(1024)(128)(4,1)S(1)}, s32[]{:S(2)}) async-start(s8[6291456]{0:T(1024)(128)(4,1)} %bitcast.133), calls=%async_computation.6 | async-start | bytes 8388608
  147.8 7.2 slice-start.1
  154.9 4.6 copy-start.5
  159.5 1.1 copy-start.6
  163.2 1.4 copy-start.3
  163.3 1.4 copy-start.17
  163.3 1.4 copy-start.18
  163.3 1.4 copy-start.19
  164.7 4.2 copy-start.10
  164.7 4.2 copy-start.15
  269.1 25.3 %copy-start.22 = (bf16[8,96]{1,0:T(8,128)(2,1)S(1)}, bf16[8,96]{1,0:T(8,128)(2,1)}, u32[]{:S(2)}) copy-start(bf16[8,96]{1,0:T(8,128)(2,1)} %reshape.299) | copy-start | bytes 4612
  295.7 0.7 copy-start.30
  295.7 8.5 copy-start.24
  299.1 466.3 %all-to-all-start.1 = ((bf16[16,1,1,32,768]{4,3,2,1,0:T(8,128)(2,1)}), bf16[16,1,1,32,768]{4,3,2,1,0:T(8,128)(2,1)}, u32[]{:S(2)}, u32[]{:S(2)}) async-start(bf16[16,1,1,32,768]{4,3,2,1,0:T(8,128)(2,1)} %bitcast.141), calls=%async_computation.1 | async-start | bytes 1572864 | tf_op jit(solution)/shard_map/all_to_all | solution.py:190
  304.2 532.4 %all-reduce.4.cloned.1.call-start = ((), (), s32[]{:S(2)}) async-start(), calls=%async_computation.4 | async-start | bytes 7087104 | tf_op jit(solution)/shard_map/psum | solution.py:224
  760.8 0.7 copy-start.20
  765.3 52.5 %all-to-all-start.3 = ((bf16[16,1,1,32,768]{4,3,2,1,0:T(8,128)(2,1)}), bf16[16,1,1,32,768]{4,3,2,1,0:T(8,128)(2,1)}, u32[]{:S(2)}, u32[]{:S(2)}) async-start(bf16[16,1,1,32,768]{4,3,2,1,0:T(8,128)(2,1)} %bitcast.142), calls=%async_computation.3 | async-start | bytes 1572864 | tf_op jit(solution)/shard_map/all_to_all | solution.py:193
Sparse Core Ops, SparseCore 0:
  295.9 456.3 all-reduce.5
  760.9 75.6 all-reduce.3
where the time goes:
time: 896 us; the launch traced here: 885 us
  waiting for transfers between devices  490 us (55%)
  local copies, waits for them, and re-layouts  209 us (23%)
  matrix products  71.2 us (8%)
  blocking collectives  42.1 us (5%)
  other arithmetic  37.1 us (4%)
  starting transfers between devices  20.9 us (2%)
  between operations  15.2 us (2%)
    unnamed x3, waiting for transfers between devices  448 us
    unnamed x92, local copies, waits for them, and re-layouts  86.3 us
    psum x1, blocking collectives, on_device(): totals = lax.psum(squares, ('clip', 'frame'))  42.1 us
    slice x6, local copies, waits for them, and re-layouts, on_device(): finished.append(summed[offset:offset + extent].reshape(local_shape))  32.6 us
    reshape x11, local copies, waits for them, and re-layouts, on_device(): item.reshape(frame_count, -1)  29.5 us
  transfers between devices with their start and end apart: 6, of which 4 were waited for; matrix products, arithmetic and copies ran while one was open for 4% of the time, Pallas kernels for 0%

commit v1 on v0

--- a/solution.py
+++ b/solution.py
@@ -1,16 +1,796 @@
+import functools
 import math
 
 import jax
 import jax.numpy as jnp
 from jax import lax
+from jax.experimental import pallas as pl
+from jax.experimental.pallas import tpu as pltpu
 from jax.sharding import PartitionSpec as P
 
 HEADS = 12
 FRAMES = 16
 TUBES = 16
-
-
 EPS = 1e-05
+
+F32 = jnp.float32
+BF16 = jnp.bfloat16
+MESH = pl.DeviceIdType.MESH
+ROW_BLOCK = 64
+
+
+def dot_nn(lhs, rhs):
+    return lax.dot_general(lhs, rhs, (((1,), (0,)), ((), ())), preferred_element_type=F32)
+
+
+def dot_nt(lhs, rhs):
+    return lax.dot_general(lhs, rhs, (((1,), (1,)), ((), ())), preferred_element_type=F32)
+
+
+def dot_tn(lhs, rhs):
+    return lax.dot_general(lhs, rhs, (((0,), (0,)), ((), ())), preferred_element_type=F32)
+
+
+def unit_norm(rows):
+    shifted = rows - jnp.mean(rows, axis=-1, keepdims=True)
+    inverse = lax.rsqrt(jnp.mean(shifted * shifted, axis=-1, keepdims=True) + EPS)
+    return shifted * inverse, inverse
+
+
+def norm_pull(scaled, unit, inverse):
+    first = jnp.mean(scaled, axis=-1, keepdims=True)
+    second = jnp.mean(scaled * unit, axis=-1, keepdims=True)
+    return inverse * (scaled - first - unit * second)
+
+
+def gelu_and_slope(hidden):
+    bell = jnp.exp(hidden * hidden * -0.5)
+    t = 1.0 / (1.0 + jnp.abs(hidden) * (0.3275911 / math.sqrt(2.0)))
+    poly = t * (
+        0.5 * 0.254829592
+        + t
+        * (
+            0.5 * -0.284496736
+            + t * (0.5 * 1.421413741 + t * (0.5 * -1.453152027 + t * (0.5 * 1.061405429)))
+        )
+    )
+    below = poly * bell
+    cumulative = jnp.where(hidden >= 0.0, 1.0 - below, below)
+    return hidden * cumulative, cumulative + hidden * bell * (1.0 / math.sqrt(2.0 * math.pi))
+
+
+def fold8(rows):
+    return jnp.sum(rows.reshape(rows.shape[0] // 8, 8, rows.shape[1]), axis=0)
+
+
+def ds(start, size, unit=None):
+    return pl.ds(pl.multiple_of(start, unit or size), size)
+
+
+class Plan:
+    def __init__(self, clips, frames, stream_shape, ff):
+        self.C, self.F, self.FF = clips, frames, ff
+        self.rows, self.spatial, self.D = stream_shape
+        self.frame_split = min(FRAMES, frames)
+        self.clip_split = frames // self.frame_split
+        self.fd = FRAMES // self.frame_split
+        self.td = TUBES // self.frame_split
+        self.cd = self.rows // self.fd
+        self.pos = self.spatial // TUBES
+        self.L = FRAMES * self.pos
+        self.S = self.cd * self.td
+        self.T = self.S * self.L
+        self.R = self.D // frames
+        self.Rh = self.R // 2
+        self.blocks = clips * frames
+        self.half = self.blocks * self.Rh
+        self.nj = ff // self.D
+        self.X = clips // 2
+        self.Y = self.X if frames % self.X == 0 else 1
+        powers = all(n & (n - 1) == 0 for n in (clips, frames, self.X, self.Y))
+        self.fits = (
+            self.clip_split == 1
+            and clips >= 2
+            and powers
+            and frames % 2 == 0
+            and self.R % 32 == 0
+            and ff == clips * self.D
+            and self.FF // 8 == self.D // 2
+            and self.pos % 16 == 0
+            and 8 % frames == 0
+        )
+
+    def steps(self, part):
+        bits = lambda n: [1 << i for i in range(n.bit_length() - 1)]
+        along_x = [("clip", 2 * b) for b in bits(self.X)]
+        along_y = [("frame", b) for b in bits(self.Y)]
+        along_z = [("frame", self.Y * b) for b in bits(self.F // self.Y)]
+        first = along_x + along_y if part == 0 else along_y + along_x
+        return [("clip", 1)] + first + along_z
+
+    def gather_steps(self):
+        return [("clip", 2 * (1 << i)) for i in range(self.X.bit_length() - 1)] + [("clip", 1)]
+
+    def place(self, part, chunk, frame):
+        clip = (chunk % self.X) * 2 + chunk // self.X
+        where = 0
+        for axis, bit in self.steps(part):
+            where = where * 2 + ((clip if axis == "clip" else frame) // bit) % 2
+        return where
+
+
+class Scatter:
+    def __init__(self, plan, me, part, held, slots, result, send_sems, recv_sems):
+        self.plan, self.me, self.held, self.slots = plan, me, held, slots
+        self.result, self.send_sems, self.recv_sems = result, send_sems, recv_sems
+        self.steps = plan.steps(part)
+        self.gather = plan.gather_steps()
+        self.at = 0
+        self.base = 0
+        self.size = plan.blocks
+        self.copies = []
+        self.slot_of_me = (me["clip"] % 2) * plan.X + me["clip"] // 2
+
+    def bit_of(self, axis, bit):
+        return (self.me[axis] // bit) % 2
+
+    def partner(self, axis, bit):
+        flipped = self.me[axis] + bit * (1 - 2 * self.bit_of(axis, bit))
+        return {**self.me, axis: flipped}
+
+    def rows(self, base, size):
+        return pl.ds(pl.multiple_of(base * self.plan.Rh, self.plan.Rh), size * self.plan.Rh)
+
+    def send(self, src, dst, axis, bit):
+        to = self.partner(axis, bit)
+        copy = pltpu.make_async_remote_copy(
+            src_ref=src,
+            dst_ref=dst,
+            send_sem=self.send_sems.at[len(self.copies)],
+            recv_sem=self.recv_sems.at[len(self.copies)],
+            device_id=(to["clip"], to["frame"]),
+            device_id_type=MESH,
+        )
+        copy.start()
+        self.copies.append(copy)
+
+    def start(self):
+        if self.at < len(self.steps):
+            axis, bit = self.steps[self.at]
+            mine = self.bit_of(axis, bit)
+            half = self.size // 2
+            self.send(
+                self.held.at[self.rows(self.base + (1 - mine) * half, half)],
+                self.slots[self.at],
+                axis,
+                bit,
+            )
+            self.base = self.base + mine * half
+            self.size = half
+        elif self.at < len(self.steps) + len(self.gather):
+            done = self.at - len(self.steps)
+            axis, bit = self.gather[done]
+            size = 1 << done
+            region = self.rows((self.slot_of_me // size) * size, size)
+            self.send(self.result.at[region], self.result.at[region], axis, bit)
+
+    def advance(self):
+        self.copies[self.at].wait_recv()
+        if self.at < len(self.steps):
+            slot = self.slots[self.at]
+            last = self.at == len(self.steps) - 1
+            target = self.result if last else self.held
+            target_base = self.slot_of_me if last else self.base
+            base, held = self.base, self.held
+
+            def add(i, _):
+                total = held[self.rows(base + i, 1)].astype(F32) + slot[self.rows(i, 1)].astype(F32)
+                target[self.rows(target_base + i, 1)] = total.astype(BF16)
+                return 0
+
+            lax.fori_loop(0, self.size, add, 0)
+        self.at += 1
+        self.start()
+
+    def finish(self):
+        while self.at < len(self.steps) + len(self.gather):
+            self.advance()
+        for copy in self.copies:
+            copy.wait_send()
+
+
+def layer_kernel(plan, refs):
+    D, T, S, L, FF, nj = plan.D, plan.T, plan.S, plan.L, plan.FF, plan.nj
+    me = {"clip": lax.axis_index("clip"), "frame": lax.axis_index("frame")}
+    frame = me["frame"]
+    hidden_tile = D // 3
+    xin, gin, n1, qkv, prob, mixed = (refs[k] for k in ("xin", "gin", "n1", "qkv", "prob", "mixed"))
+    mid, n2, act, slope, obuf, acc = (refs[k] for k in ("mid", "n2", "act", "slope", "obuf", "acc"))
+    dmid, sums, rows_ref = refs["dmid"], refs["sums"], refs["rows"]
+    wqkv, wout, wup, wdown = (refs[k] for k in ("wqkv", "wout", "wup", "wdown"))
+    dbranch, dmixed, igbuf = n2, mixed, obuf
+
+    def row(i):
+        return rows_ref[pl.ds(i, 1), :]
+
+    loads = []
+    for i, (src, dst) in enumerate(
+        [
+            (refs["wqkv_h"], wqkv),
+            (refs["wout_h"], wout),
+            (refs["wup_h"], wup),
+            (refs["wdown_h"].at[pl.ds(0, FF // 2)], wdown.at[0]),
+            (refs["wdown_h"].at[pl.ds(FF // 2, FF // 2)], wdown.at[1]),
+        ]
+    ):
+        load = pltpu.make_async_copy(src, dst, refs["load_sems"].at[i])
+        load.start()
+        loads.append(load)
+
+    barrier = pltpu.get_barrier_semaphore()
+    greeted = [(me["clip"], lax.rem(frame + i, plan.F)) for i in range(1, plan.F)]
+    for axis, bit in plan.gather_steps():
+        flipped = me[axis] + bit * (1 - 2 * ((me[axis] // bit) % 2))
+        greeted.append((flipped, frame))
+    for peer in greeted:
+        pl.semaphore_signal(barrier, inc=1, device_id=peer, device_id_type=MESH)
+    pl.semaphore_wait(barrier, len(greeted))
+
+    def tubes(n, device):
+        clip_set, tube = n // plan.td, n % plan.td
+        return clip_set, ds((device * plan.td + tube) * plan.pos, plan.pos)
+
+    sends = []
+
+    def to_tubes(which, source, target, n):
+        arriving = []
+        for i in range(plan.F):
+            peer = lax.rem(frame + i, plan.F)
+            clip_set, positions = tubes(n, peer)
+            src = source.at[:, clip_set, positions]
+            dst = target.at[n, pl.ds(frame * plan.fd, plan.fd)]
+            recv = refs["a2a_recv"].at[which, n, i]
+            if i == 0:
+                copy = pltpu.make_async_copy(src, dst, recv)
+                copy.start()
+                arriving.append(copy.wait)
+            else:
+                copy = pltpu.make_async_remote_copy(
+                    src_ref=src,
+                    dst_ref=dst,
+                    send_sem=refs["a2a_send"].at[which, n, i],
+                    recv_sem=recv,
+                    device_id=(me["clip"], peer),
+                    device_id_type=MESH,
+                )
+                copy.start()
+                sends.append(copy.wait_send)
+                arriving.append(copy.wait_recv)
+        return arriving
+
+    def to_frames(which, source, target, n):
+        arriving = []
+        for i in range(plan.F):
+            peer = lax.rem(frame + i, plan.F)
+            clip_set, positions = tubes(n, frame)
+            src = source.at[n, pl.ds(peer * plan.fd, plan.fd)]
+            dst = target.at[:, clip_set, positions]
+            recv = refs["a2a_recv"].at[which, n, i]
+            if i == 0:
+                copy = pltpu.make_async_copy(src, dst, recv)
+                copy.start()
+                arriving.append((lambda: None, copy.wait))
+            else:
+                copy = pltpu.make_async_remote_copy(
+                    src_ref=src,
+                    dst_ref=dst,
+                    send_sem=refs["a2a_send"].at[which, n, i],
+                    recv_sem=recv,
+                    device_id=(me["clip"], peer),
+                    device_id_type=MESH,
+                )
+                copy.start()
+                arriving.append((copy.wait_recv, copy.wait_send))
+        return arriving
+
+    def wait_all(waits):
+        for wait in waits:
+            wait()
+
+    x_arrives = [to_tubes(0, refs["stream"], xin, n) for n in range(S)]
+    g_arrives = [to_tubes(1, refs["grad"], gin, n) for n in range(S)]
+
+    scatters = {}
+    for group in range(3):
+        for part in range(2):
+            at = group * 2 + part
+            scatters[group, part] = Scatter(
+                plan,
+                me,
+                part,
+                refs["groups"][group].at[part],
+                refs["slots"][at],
+                refs["res"].at[at],
+                refs["rs_send"].at[at],
+                refs["rs_recv"].at[at],
+            )
+
+    def start(group):
+        for part in range(2):
+            scatters[group, part].start()
+
+    def advance(group):
+        for part in range(2):
+            scatters[group, part].advance()
+
+    def seq_rows(ref, s, start, size):
+        frames = size // plan.pos
+        block = ref[s, pl.ds(start // plan.pos, frames)]
+        return block.reshape(size, D)
+
+    sums[...] = jnp.zeros_like(sums)
+
+    def tally(i, value):
+        sums[i] += fold8(value)
+
+    lanes = lax.broadcasted_iota(jnp.int32, (1, 128), 1)
+    head_masks = [(lanes < 64).astype(BF16), (lanes >= 64).astype(BF16)]
+    scale = 1.0 / math.sqrt(D // HEADS)
+
+    for s in range(S):
+        wait_all(x_arrives[s])
+
+        def first_norm(i, _):
+            x = seq_rows(xin, s, i * ROW_BLOCK, ROW_BLOCK).astype(F32)
+            unit, _ = unit_norm(x)
+            tally(8, x * x)
+            n1[ds(s * L + i * ROW_BLOCK, ROW_BLOCK), :] = (unit * row(0) + row(1)).astype(BF16)
+            return 0
+
+        lax.fori_loop(0, L // ROW_BLOCK, first_norm, 0)
+        if s == 0:
+            loads[0].wait()
+        tokens = pl.ds(s * L, L)
+        for third in range(3):
+
+            def project(i, _):
+                column = third * D + i * hidden_tile
+                out = dot_nn(n1[tokens, :], wqkv[:, ds(column, hidden_tile)])
+                if third != 1:
+                    bias = rows_ref[pl.ds(2 + third // 2, 1), ds(i * hidden_tile, hidden_tile)]
+                    out = out + bias
+                if third == 0:
+                    out = out * scale
+                qkv[third, tokens, ds(i * hidden_tile, hidden_tile)] = out.astype(BF16)
+                return 0
+
+            lax.fori_loop(0, D // hidden_tile, project, 0)
+
+        def attend(pair, _):
+            columns = ds(pair * 128, 128)
+            q = qkv[0, tokens, columns]
+            k = qkv[1, tokens, columns]
+            v = qkv[2, tokens, columns]
+            out = jnp.zeros((L, 128), F32)
+            for e in range(2):
+                scores = dot_nt(q * head_masks[e], k)
+                power = jnp.exp(scores - jnp.max(scores, axis=-1, keepdims=True))
+                share = 1.0 / jnp.sum(power, axis=-1, keepdims=True)
+                weight = (power * share).astype(BF16)
+                prob[s * HEADS + pair * 2 + e] = weight
+                out = out + dot_nn(weight, v * head_masks[e])
+            mixed[tokens, columns] = out.astype(BF16)
+            return 0
+
+        lax.fori_loop(0, HEADS // 2, attend, 0)
+
+    loads[1].wait()
+
+    def project_out(i, _):
+        columns = ds(i * hidden_tile, hidden_tile)
+        mid[:, columns] = dot_nn(mixed[...], wout[:, columns]) + rows_ref[pl.ds(4, 1), columns]
+        return 0
+
+    lax.fori_loop(0, D // hidden_tile, project_out, 0)
+    for s in range(S):
+
+        def second_norm(i, _):
+            rows = ds(s * L + i * ROW_BLOCK, ROW_BLOCK)
+            branch = mid[rows, :]
+            middle = seq_rows(xin, s, i * ROW_BLOCK, ROW_BLOCK).astype(F32) + branch
+            mid[rows, :] = middle
+            tally(9, middle * middle)
+            tally(11, branch * branch)
+            unit, _ = unit_norm(middle)
+            n2[rows, :] = (unit * row(5) + row(6)).astype(BF16)
+            return 0
+
+        lax.fori_loop(0, L // ROW_BLOCK, second_norm, 0)
+
+    loads[2].wait()
+
+    def up(i, _):
+        j, part = i // 3, i % 3
+        columns = ds(part * hidden_tile, hidden_tile)
+        bias = rows_ref[pl.ds(8 + j, 1), columns]
+        hidden = dot_nn(n2[...], wup[:, ds(i * hidden_tile, hidden_tile)]) + bias
+        active, steep = gelu_and_slope(hidden)
+        act[ds(j * T, T), columns] = active.astype(BF16)
+        slope[ds(j * T, T), columns] = steep.astype(BF16)
+        return 0
+
+    lax.fori_loop(0, FF // hidden_tile, up, 0)
+    loads[3].wait()
+    loads[4].wait()
+    out_arrives = []
+    for s in range(S):
+
+        def down(i, _):
+            columns = ds(i * hidden_tile, hidden_tile)
+            total = rows_ref[pl.ds(7, 1), columns]
+            for j in range(nj):
+                per = nj // 2
+                total = total + dot_nn(
+                    act[pl.ds(j * T + s * L, L), :],
+                    wdown[j // per, pl.ds((j % per) * D, D), columns],
+                )
+            result = total + mid[pl.ds(s * L, L), columns]
+            sums[10, :, columns] += fold8(result * result)
+            sums[12, :, columns] += fold8(total * total)
+            obuf[s, :, :, columns] = result.astype(BF16).reshape(FRAMES, plan.pos, hidden_tile)
+            return 0
+
+        lax.fori_loop(0, D // hidden_tile, down, 0)
+        out_arrives += to_frames(2, obuf, refs["out_h"], s)
+
+    for s in range(S):
+        wait_all(g_arrives[s])
+    wide = D // 2
+
+    def put(group, chunk, frame_block, block):
+        for part in range(2):
+            at = plan.place(part, chunk, frame_block)
+            rows = pl.ds(pl.multiple_of(at * plan.Rh, plan.Rh), plan.Rh)
+            piece = block[part * plan.Rh : (part + 1) * plan.Rh]
+            refs["groups"][group][part, rows, :] = piece.astype(BF16)
+
+    g_rows = gin[...].reshape(T, D)
+
+    def grad_down(i, _):
+        a = act[ds((i // 2) * T, T), ds((i % 2) * wide, wide)]
+        out = dot_tn(a, gin[...].reshape(T, D))
+        per = 8 // plan.F
+        for c in range(plan.C):
+            put(0, c, i // per, out[c * plan.R : (c + 1) * plan.R])
+        return 0
+
+    del g_rows
+    lax.fori_loop(0, FF // wide, grad_down, 0)
+    start(0)
+
+    def through_gelu(i, _):
+        j, part = i // 3, i % 3
+        columns = ds(part * hidden_tile, hidden_tile)
+        per = nj // 2
+        rows = ds((j % per) * D + part * hidden_tile, hidden_tile)
+        d_active = dot_nt(gin[...].reshape(T, D), wdown[j // per, rows, :])
+        d_hidden = (d_active * slope[ds(j * T, T), columns].astype(F32)).astype(BF16)
+        slope[ds(j * T, T), columns] = d_hidden
+        sums[13 + j, :, columns] += fold8(d_hidden.astype(F32))
+        return 0
+
+    lax.fori_loop(0, FF // hidden_tile, through_gelu, 0)
+    advance(0)
+
+    def grad_columns(group, chunk, lhs, rhs):
+        def half(m, _):
+            out = dot_tn(lhs(ds(m * wide, wide)), rhs())
+            for f in range(plan.F // 2):
+                put(group, chunk, m * (plan.F // 2) + f, out[f * plan.R : (f + 1) * plan.R])
+            return 0
+
+        lax.fori_loop(0, 2, half, 0)
+
+    def grad_up(c, _):
+        grad_columns(
+            1, c, lambda columns: n2[:, columns], lambda: slope[ds(c * T, T), :]
+        )
+        return 0
+
+    lax.fori_loop(0, plan.C, grad_up, 0)
+    start(1)
+
+    def d_two(i, _):
+        rows = ds(i * hidden_tile, hidden_tile)
+        total = jnp.zeros((T, hidden_tile), F32)
+        for j in range(nj):
+            total = total + dot_nt(slope[pl.ds(j * T, T), :], wup[rows, pl.ds(j * D, D)])
+        acc[:, rows] = total
+        return 0
+
+    lax.fori_loop(0, D // hidden_tile, d_two, 0)
+    advance(1)
+
+    for s in range(S):
+
+        def second_norm_back(i, _):
+            rows = ds(s * L + i * ROW_BLOCK, ROW_BLOCK)
+            up_grad = acc[rows, :]
+            unit, inverse = unit_norm(mid[rows, :])
+            g = seq_rows(gin, s, i * ROW_BLOCK, ROW_BLOCK).astype(F32)
+            d_middle = g + norm_pull(up_grad * row(5), unit, inverse)
+            dmid[rows, :] = d_middle
+            low = d_middle.astype(BF16)
+            dbranch[rows, :] = low
+            tally(4, low.astype(F32))
+            tally(5, up_grad * unit)
+            tally(6, up_grad)
+            tally(7, g)
+            return 0
+
+        lax.fori_loop(0, L // ROW_BLOCK, second_norm_back, 0)
+
+    advance(0)
+    last = plan.C - 1
+    grad_columns(2, last, lambda columns: mixed[:, columns], lambda: dbranch[...])
+
+    def through_out(i, _):
+        columns = ds(i * hidden_tile, hidden_tile)
+        dmixed[:, columns] = dot_nt(dbranch[...], wout[columns, :]).astype(BF16)
+        return 0
+
+    lax.fori_loop(0, D // hidden_tile, through_out, 0)
+
+    for s in range(S):
+        tokens = pl.ds(s * L, L)
+
+        def attend_back(pair, _):
+            columns = ds(pair * 128, 128)
+            q = qkv[0, tokens, columns]
+            k = qkv[1, tokens, columns]
+            v = qkv[2, tokens, columns]
+            d_out = dmixed[tokens, columns]
+            zero = jnp.zeros((L, 128), F32)
+            d_q, d_k, d_v = zero, zero, zero
+            for e in range(2):
+                weight = prob[s * HEADS + pair * 2 + e]
+                own = d_out * head_masks[e]
+                d_weight = dot_nt(own, v)
+                d_v = d_v + dot_tn(weight, own)
+                wide_weight = weight.astype(F32)
+                centre = jnp.sum(wide_weight * d_weight, axis=-1, keepdims=True)
+                d_score = (wide_weight * (d_weight - centre)).astype(BF16)
+                d_q = d_q + dot_nn(d_score, k * head_masks[e])
+                d_k = d_k + dot_tn(d_score, q * head_masks[e])
+            qkv[0, tokens, columns] = (d_q * scale).astype(BF16)
+            qkv[1, tokens, columns] = d_k.astype(BF16)
+            qkv[2, tokens, columns] = d_v.astype(BF16)
+            return 0
+
+        lax.fori_loop(0, HEADS // 2, attend_back, 0)
+        advance(s % 2)
+
+    def grad_qkv(c, _):
+        grad_columns(2, c, lambda columns: n1[:, columns], lambda: qkv[c])
+        return 0
+
+    lax.fori_loop(0, 3, grad_qkv, 0)
+    start(2)
+
+    def d_one(i, _):
+        rows = ds(i * hidden_tile, hidden_tile)
+        total = jnp.zeros((T, hidden_tile), F32)
+        for j in range(3):
+            total = total + dot_nt(qkv[j], wqkv[rows, pl.ds(j * D, D)])
+        acc[:, rows] = total
+        return 0
+
+    lax.fori_loop(0, D // hidden_tile, d_one, 0)
+    advance(2)
+    for recv, send in out_arrives:
+        send()
+    in_arrives = []
+    for s in range(S):
+
+        def first_norm_back(i, _):
+            rows = ds(s * L + i * ROW_BLOCK, ROW_BLOCK)
+            up_grad = acc[rows, :]
+            x = seq_rows(xin, s, i * ROW_BLOCK, ROW_BLOCK).astype(F32)
+            unit, inverse = unit_norm(x)
+            total = dmid[rows, :] + norm_pull(up_grad * row(0), unit, inverse)
+            frames = ROW_BLOCK // plan.pos
+            igbuf[s, pl.ds(i * frames, frames)] = total.astype(BF16).reshape(frames, plan.pos, D)
+            tally(0, up_grad * unit)
+            tally(1, up_grad)
+            tally(2, qkv[0, rows, :].astype(F32))
+            tally(3, qkv[2, rows, :].astype(F32))
+            return 0
+
+        lax.fori_loop(0, L // ROW_BLOCK, first_norm_back, 0)
+        in_arrives += to_frames(3, igbuf, refs["ig_h"], s)
+
+    vbuf, vrecv = refs["vbuf"], refs["vrecv"]
+    count = sums.shape[0]
+    for i in range(count):
+        vbuf[0, pl.ds(i, 1), :] = jnp.sum(sums[i], axis=0, keepdims=True)
+    hops = plan.steps(0)
+    small = []
+    for i, (axis, bit) in enumerate(hops):
+        flipped = me[axis] + bit * (1 - 2 * ((me[axis] // bit) % 2))
+        to = {**me, axis: flipped}
+        copy = pltpu.make_async_remote_copy(
+            src_ref=vbuf.at[i],
+            dst_ref=vrecv.at[i],
+            send_sem=refs["v_send"].at[i],
+            recv_sem=refs["v_recv"].at[i],
+            device_id=(to["clip"], to["frame"]),
+            device_id_type=MESH,
+        )
+        copy.start()
+        small.append(copy)
+        if i == 0:
+            advance(0)
+            advance(1)
+        elif i % 2 == 0:
+            advance(2)
+        copy.wait_recv()
+        vbuf[i + 1] = vbuf[i] + vrecv[i]
+    refs["vec"][...] = vbuf[len(hops)]
+    for copy in small:
+        copy.wait_send()
+    for group in (0, 1, 2):
+        for part in range(2):
+            scatters[group, part].finish()
+    for recv, send in out_arrives:
+        recv()
+    for recv, send in in_arrives:
+        send()
+        recv()
+    wait_all(sends)
+
+
+def fused(plan, stream, masked, weights, rows):
+    D, T, S, L, FF = plan.D, plan.T, plan.S, plan.L, plan.FF
+    n_steps = len(plan.steps(0))
+    n_hops = n_steps + len(plan.gather_steps())
+    n_vec = 13 + plan.nj
+    vec_rows = -(-n_vec // 8) * 8
+    vmem = lambda shape, kind=BF16: pltpu.VMEM(shape, kind)
+    scratch = {
+        "wqkv": vmem((D, 3 * D)),
+        "wout": vmem((D, D)),
+        "wup": vmem((D, FF)),
+        "wdown": vmem((2, FF // 2, D)),
+        "xin": vmem((S, FRAMES, plan.pos, D)),
+        "gin": vmem((S, FRAMES, plan.pos, D)),
+        "n1": vmem((T, D)),
+        "qkv": vmem((3, T, D)),
+        "prob": vmem((S * HEADS, L, L)),
+        "mixed": vmem((T, D)),
+        "mid": vmem((T, D), F32),
+        "n2": vmem((T, D)),
+        "act": vmem((plan.nj * T, D)),
+        "slope": vmem((plan.nj * T, D)),
+        "obuf": vmem((S, FRAMES, plan.pos, D)),
+        "acc": vmem((T, D), F32),
+        "dmid": vmem((T, D), F32),
+        "sums": vmem((n_vec, 8, D), F32),
+        "g_down": vmem((2, plan.half, D)),
+        "g_up": vmem((2, plan.half, D)),
+        "vbuf": vmem((n_steps + 1, vec_rows, D), F32),
+        "vrecv": vmem((n_steps, vec_rows, D), F32),
+        "load_sems": pltpu.SemaphoreType.DMA((5,)),
+        "a2a_send": pltpu.SemaphoreType.DMA((4, S, plan.F)),
+        "a2a_recv": pltpu.SemaphoreType.DMA((4, S, plan.F)),
+        "rs_send": pltpu.SemaphoreType.DMA((6, n_hops)),
+        "rs_recv": pltpu.SemaphoreType.DMA((6, n_hops)),
+        "v_send": pltpu.SemaphoreType.DMA((n_steps,)),
+        "v_recv": pltpu.SemaphoreType.DMA((n_steps,)),
+    }
+    for i in range(n_steps):
+        scratch[f"slot{i}"] = vmem((4 if i == 0 else 6, plan.half >> (i + 1), D))
+    names_in = ["stream", "grad", "wqkv_h", "wout_h", "wup_h", "wdown_h", "rows"]
+    names_out = ["out_h", "ig_h", "res", "vec"]
+    names = names_in + names_out + list(scratch)
+
+    def kernel(*args):
+        refs = dict(zip(names, args))
+        refs["groups"] = (refs["g_down"], refs["g_up"], refs["wdown"])
+        refs["slots"] = []
+        for at in range(6):
+            first = (
+                refs["slot0"].at[at]
+                if at < 4
+                else refs["act"].at[pl.ds((at - 4) * (plan.half // 2), plan.half // 2)]
+            )
+            later = [refs[f"slot{i}"].at[at] for i in range(1, n_steps)]
+            refs["slots"].append([first] + later)
+        layer_kernel(plan, refs)
+
+    hbm = pl.BlockSpec(memory_space=pl.ANY)
+    in_vmem = pl.BlockSpec(memory_space=pltpu.VMEM)
+    token_shape = (plan.fd, plan.cd, plan.spatial, D)
+    out = pl.pallas_call(
+        kernel,
+        out_shape=(
+            jax.ShapeDtypeStruct(token_shape, BF16),
+            jax.ShapeDtypeStruct(token_shape, BF16),
+            jax.ShapeDtypeStruct((6, plan.C * plan.Rh, D), BF16),
+            jax.ShapeDtypeStruct((vec_rows, D), F32),
+        ),
+        in_specs=[hbm] * 6 + [in_vmem],
+        out_specs=(hbm, hbm, in_vmem, in_vmem),
+        scratch_shapes=list(scratch.values()),
+        compiler_params=pltpu.CompilerParams(
+            collective_id=0, has_side_effects=True, vmem_limit_bytes=VMEM_LIMIT
+        ),
+        name="tube_layer",
+    )(stream.reshape(token_shape), masked.reshape(token_shape), *weights, rows)
+    return out
+
+
+VMEM_LIMIT = 64 * 1024 * 1024 - 512 * 1024
+
+
+def with_kernel(
+    plan,
+    stream,
+    out_grad,
+    token_mask,
+    ln1_gain,
+    ln1_bias,
+    w_qkv,
+    b_qv,
+    w_out,
+    b_out,
+    ln2_gain,
+    ln2_bias,
+    w_up,
+    b_up,
+    w_down,
+    b_down,
+):
+    D, C, R, Rh = plan.D, plan.C, plan.R, plan.Rh
+    masked = jnp.where(token_mask[:, :, None] == 1, out_grad, jnp.zeros((), BF16))
+    small = [ln1_gain, ln1_bias, b_qv, b_out, ln2_gain, ln2_bias, b_down, b_up]
+    rows = jnp.concatenate(small).reshape(8 + plan.nj, D)
+    output, input_grad, gathered, totals = fused(
+        plan, stream, masked, (w_qkv, w_out, w_up, w_down), rows
+    )
+    gathered = gathered.reshape(3, 2, C, Rh, D).astype(F32)
+    g_down = jnp.transpose(gathered[0], (1, 0, 2, 3)).reshape(C * R, D)
+    by_row = lambda group: jnp.transpose(gathered[group], (0, 2, 1, 3))
+    g_up = by_row(1).reshape(R, C * D)
+    projections = by_row(2)
+    g_qkv = projections[:, :, :3].reshape(R, 3 * D)
+    g_out = projections[:, :, 3].reshape(R, D)
+    frame = lax.axis_index("frame")
+
+    def own(first, count=1):
+        flat = totals[first : first + count].reshape(-1)
+        share = count * D // plan.F
+        return lax.dynamic_slice(flat, (frame * share,), (share,))
+
+    entries = plan.T * D * C * plan.F
+    squares = jnp.sum(totals[8:13], axis=-1)
+    statistics = jnp.sqrt(squares / entries)
+    return (
+        output.reshape(stream.shape),
+        input_grad.reshape(stream.shape),
+        own(0),
+        own(1),
+        g_qkv,
+        own(2, 2),
+        g_out,
+        own(4),
+        own(5),
+        own(6),
+        g_up,
+        own(13, plan.nj),
+        g_down,
+        own(7),
+        statistics,
+    )
 
 
 def layer_norm(inputs, norm_gain, norm_shift):
@@ -35,7 +815,7 @@
     return cumulative + hidden_state * density
 
 
-def on_device(
+def with_collectives(
     stream,
     out_grad,
     token_mask,
@@ -249,38 +1029,33 @@
 
 
 def solution(mesh):
-    in_specs = (
-        P(("clip", "frame"), None, None),
-        P(("clip", "frame"), None, None),
-        P(("clip", "frame"), None),
-        P(),
-        P(),
-        P(),
-        P(),
-        P(),
-        P(),
-        P(),
-        P(),
-        P(),
-        P(),
-        P(),
-        P(),
-    )
+    clips, frames = mesh.shape["clip"], mesh.shape["frame"]
+
+    def on_device(stream, *rest):
+        ff = rest[-4].shape[1]
+        plan = Plan(clips, frames, stream.shape, ff)
+        if plan.fits:
+            return with_kernel(plan, stream, *rest)
+        return with_collectives(stream, *rest)
+
+    tokens = P(("clip", "frame"), None, None)
+    in_specs = (tokens, tokens, P(("clip", "frame"), None)) + (P(),) * 12
+    rows, vector = P("frame", None), P("frame")
     out_specs = (
-        P(("clip", "frame"), None, None),
-        P(("clip", "frame"), None, None),
-        P("frame"),
-        P("frame"),
-        P("frame", None),
-        P("frame"),
-        P("frame", None),
-        P("frame"),
-        P("frame"),
-        P("frame"),
-        P("frame", None),
-        P("frame"),
-        P("frame", None),
-        P("frame"),
+        tokens,
+        tokens,
+        vector,
+        vector,
+        rows,
+        vector,
+        rows,
+        vector,
+        vector,
+        vector,
+        rows,
+        vector,
+        rows,
+        vector,
         P(),
     )
     return jax.shard_map(

time: 896 us -> 218 us (0.24); the launches traced: 885 us -> 217 us
  waiting for transfers between devices: 490 us -> 0 us
  Pallas kernels: 0 us -> 191 us
  local copies, waits for them, and re-layouts: 209 us -> 21.6 us
  matrix products: 71.2 us -> 0 us
  blocking collectives: 42.1 us -> 0 us
  other arithmetic: 37.1 us -> 4.22 us
  starting transfers between devices: 20.9 us -> 0 us
  between operations: 15.2 us -> 0.7 us
    unnamed x3 -> x0, waiting for transfers between devices: 448 us -> none
    pallas_call x0 -> x1, Pallas kernels: none -> 191 us  [fused(): pl.pallas_call(kernel, out_shape=(jax.ShapeDtypeStruct(token_shape, BF16)...]
    unnamed x92 -> x16, local copies, waits for them, and re-layouts: 86.3 us -> 9.96 us
    dot_general x18 -> x0, matrix products: 71.2 us -> none  [the longest x1 16 us: on_device(): jnp.dot(second_normed_input, w_up, preferred_element_type=jnp.float32)]
    reshape x23 -> x3, local copies, waits for them, and re-layouts: 56.4 us -> 0.65 us  [the longest x1 0.63 us: with_kernel(): rows = jnp.concatenate(small).reshape(8 + plan.nj, D)]
    psum x1 -> x0, blocking collectives: 42.1 us -> none  [on_device(): totals = lax.psum(squares, ('clip', 'frame'))]
    slice x12 -> x5, local copies, waits for them, and re-layouts: 42.2 us -> 4.55 us  [the longest x3 2.52 us: own(): flat = totals[first:first + count].reshape(-1)]
    all_to_all x4 -> x0, waiting for transfers between devices: 25.2 us -> none  [the longest x1 16.3 us: on_device(): lax.all_to_all(leaving(stream), 'frame', split_axis=2, concat_axis=0, til...]
  transfers between devices with their start and end apart: 6 -> 0, of which waited for: 4 -> 0; matrix products, arithmetic and copies ran while one was open for 4% -> 0% of each run, Pallas kernels for 0% -> 0%
where the time goes in v1:
time: 218 us; the launch traced here: 217 us
  Pallas kernels  191 us (88%)
  local copies, waits for them, and re-layouts  21.6 us (10%)
  other arithmetic  4.22 us (2%)
    pallas_call x1, Pallas kernels, fused(): pl.pallas_call(kernel, out_shape=(jax.ShapeDtypeStruct(token_shape, BF16)...  191 us
    unnamed x16, local copies, waits for them, and re-layouts  9.96 us

profile of v1, /device:TPU:1, one launch (start us, length us, event | category | flops | bytes accessed | tf_op | source)
XLA Modules:
  0.0 217.2 jit_solution(18169042941283012575)
XLA Ops:
  0.7 0.7 broadcast_compare_fusion
  1.3 0.7 constant_dynamic-update-slice_fusion.7
  2.0 0.7 constant_dynamic-update-slice_fusion.6
  2.7 0.7 constant_dynamic-update-slice_fusion.5
  3.4 0.7 constant_dynamic-update-slice_fusion.4
  4.1 0.7 constant_dynamic-update-slice_fusion.3
  4.8 0.7 constant_dynamic-update-slice_fusion.2
  5.5 0.7 constant_dynamic-update-slice_fusion.1
  6.2 0.7 constant_dynamic-update-slice_fusion
  6.9 0.6 reshape.84.args_6_
  7.5 2.1 select_bitcast_fusion.args_1_
  9.7 190.7 %tube_layer.1 = (bf16[2,1,256,768]{3,2,1,0:T(8,128)(2,1)}, bf16[2,1,256,768]{3,2,1,0:T(8,128)(2,1)}, bf16[6,192,768]{2,1,0:T(8,128)(2,1)}, f32[24,768]{1,0:T(8,128)}) custom-call(bf16[2,1,256,768]{3,2,1,0:T(8,128)(2,1)} %bitcast.45, bf16[2,1,256,768]{3,2,1,0:T(8,128)(2,1)} %select_bitcast_fusion.args_1_, bf16[768,2304]{1,0:T(8,128)(2,1)} %args_2_.4, ...), custom_call_target="tpu_custom_call" | custom-call | tf_op jit(solution)/shard_map/tube_layer/pallas_call | solution.py:713
  200.4 0.9 slice_reduce_fusion
  201.2 0.5 multiply_sqrt_fusion
  201.8 0.7 slice.49
  202.5 0.6 dynamic_slice.40
  203.1 0.8 slice.55
  204.0 1.0 fusion.7
  204.9 0.6 fusion.4
  205.5 0.7 dynamic_slice.47
  206.2 0.6 fusion.2
  206.8 0.6 fusion
  207.4 1.7 fusion.6
  209.1 1.1 copy.35
  210.2 0.8 copy.34
  211.0 1.2 copy.38
  212.2 0.8 copy.40
  212.9 0.3 slice.61
  213.3 0.7 copy.36
  214.0 0.0 copy-start.1
  214.0 1.1 copy.37
  215.1 0.0 copy-start
  215.1 0.2 copy-done.1
  215.3 0.9 copy.51
  216.2 0.1 copy-done
  216.3 0.9 copy.52
  (3 shorter events, 0.0 us)
Async XLA Ops:
  214.0 1.3 copy-start.1
  215.1 1.2 copy-start

commit v2 on v1

v2 whole, which is shorter than its diff:
```python
import functools
import math
from types import SimpleNamespace

import jax
import jax.numpy as jnp
from jax import lax
from jax.experimental import pallas as pl
from jax.experimental.pallas import tpu as pltpu
from jax.sharding import PartitionSpec as P

HEADS = 12
FRAMES = 16
TUBES = 16
EPS = 1e-05

F32 = jnp.float32
BF16 = jnp.bfloat16
MESH = pl.DeviceIdType.MESH
ROW_BLOCK = 64
CLIP = "clip"
FRAME = "frame"


SIXTHS = 6
SHARES = (
    (("yzx", 2), ("xyz", 2), ("zyx", 2),),
    (("yxz", 2), ("xzy", 2), ("xyz", 2),),
    (("xzy", 2), ("yxz", 2), ("xyz", 2),),
)
DUE = dict(
    GU1=(0,),
    GU2=(1,),
    GU3=(2,),
    DM=(3, 4),
    AB00=(5,),
    AB01=(0, 1),
    AB10=(2,),
    D1=(0, 3, 4),
    L11=(1,),
    V0=(6, 7, 8, 2, 5),
    V1=(0, 4, 3, 6, 1, 7, 2, 8, 5, 0),
    V2=(3, 4, 8, 7, 6, 2, 0, 1, 4),
    V3=(0, 5, 2, 1, 2, 3, 4, 1, 8, 4, 3, 7, 3, 6),
    V4=(5, 6, 8, 7, 5, 6, 5, 8, 6),
    END=(7, 8, 7),
)


def dot_nn(lhs, rhs):
    return lax.dot_general(lhs, rhs, (((1,), (0,)), ((), ())), preferred_element_type=F32)


def dot_nt(lhs, rhs):
    return lax.dot_general(lhs, rhs, (((1,), (1,)), ((), ())), preferred_element_type=F32)


def dot_tn(lhs, rhs):
    return lax.dot_general(lhs, rhs, (((0,), (0,)), ((), ())), preferred_element_type=F32)


def unit_norm(rows):
    shifted = rows - jnp.mean(rows, axis=-1, keepdims=True)
    inverse = lax.rsqrt(jnp.mean(shifted * shifted, axis=-1, keepdims=True) + EPS)
    return shifted * inverse, inverse


def norm_pull(scaled, unit, inverse):
    first = jnp.mean(scaled, axis=-1, keepdims=True)
    second = jnp.mean(scaled * unit, axis=-1, keepdims=True)
    return inverse * (scaled - first - unit * second)


def gelu_and_slope(hidden):
    bell = jnp.exp(hidden * hidden * -0.5)
    t = 1.0 / (1.0 + jnp.abs(hidden) * (0.3275911 / math.sqrt(2.0)))
    poly = t * (
        0.5 * 0.254829592
        + t
        * (
            0.5 * -0.284496736
            + t * (0.5 * 1.421413741 + t * (0.5 * -1.453152027 + t * (0.5 * 1.061405429)))
        )
    )
    below = poly * bell
    cumulative = jnp.where(hidden >= 0.0, 1.0 - below, below)
    return hidden * cumulative, cumulative + hidden * bell * (1.0 / math.sqrt(2.0 * math.pi))


def fold8(rows):
    return jnp.sum(rows.reshape(rows.shape[0] // 8, 8, rows.shape[1]), axis=0)


def ds(start, size, unit=None):
    return pl.ds(pl.multiple_of(start, unit or size), size)


class Plan:
    def __init__(self, clips, frames, stream_shape, ff):
        self.C, self.F, self.FF = clips, frames, ff
        self.rows, self.spatial, self.D = stream_shape
        self.frame_split = min(FRAMES, frames)
        self.clip_split = frames // self.frame_split
        self.fd = FRAMES // self.frame_split
        self.td = TUBES // self.frame_split
        self.cd = self.rows // self.fd
        self.pos = self.spatial // TUBES
        self.L = FRAMES * self.pos
        self.S = self.cd * self.td
        self.T = self.S * self.L
        self.R = self.D // frames
        self.blocks = clips * frames
        self.whole = self.blocks * self.R
        self.parts = []
        for group, shares in enumerate(SHARES):
            first = 0
            for part, (order, share) in enumerate(shares):
                rows = self.R * share // SIXTHS
                self.parts.append((group, order, first, rows))
                first += rows
        self.nj = ff // self.D
        self.X = clips // 2
        self.Y = self.X if frames % self.X == 0 else 1
        powers = all(n & (n - 1) == 0 for n in (clips, frames, self.X, self.Y))
        self.fits = (
            self.clip_split == 1
            and clips >= 2
            and powers
            and frames % 2 == 0
            and self.R % (16 * SIXTHS) == 0
            and ff == clips * self.D
            and self.pos % 16 == 0
            and self.D % (ff // frames) == 0
        )

    def steps(self, order):
        bits = lambda n: [1 << i for i in range(n.bit_length() - 1)]
        along = dict(
            x=[(CLIP, 2 * b) for b in bits(self.X)],
            y=[(FRAME, b) for b in bits(self.Y)],
            z=[(FRAME, self.Y * b) for b in bits(self.F // self.Y)],
        )
        return [(CLIP, 1)] + along[order[0]] + along[order[1]] + along[order[2]]

    def gather_steps(self):
        return [(CLIP, 2 * (1 << i)) for i in range(self.X.bit_length() - 1)] + [(CLIP, 1)]

    def place(self, order, chunk, frame):
        clip = (chunk % self.X) * 2 + chunk // self.X
        where = 0
        for axis, bit in self.steps(order):
            where = where * 2 + ((clip if axis == CLIP else frame) // bit) % 2
        return where


class Scatter:
    def __init__(self, plan, me, part, held, slots, results, send_sems, recv_sems):
        group, order, first, self.height = plan.parts[part]
        self.plan, self.me = plan, me
        self.steps = plan.steps(order)
        self.gather = plan.gather_steps()
        rows = lambda count, per: pl.ds(first * per, count * per)
        self.held = held.at[rows(self.height, plan.blocks)]
        self.slots = [
            slot.at[rows(self.height, plan.blocks >> (i + 1))] for i, slot in enumerate(slots)
        ]
        self.result = results.at[rows(self.height, plan.C)]
        self.send_sems, self.recv_sems = send_sems.at[part], recv_sems.at[part]
        self.at = 0
        self.base = 0
        self.size = plan.blocks
        self.copies = []
        self.slot_of_me = (me[CLIP] % 2) * plan.X + me[CLIP] // 2

    def bit_of(self, axis, bit):
        return (self.me[axis] // bit) % 2

    def partner(self, axis, bit):
        flipped = self.me[axis] + bit * (1 - 2 * self.bit_of(axis, bit))
        return {**self.me, axis: flipped}

    def rows(self, base, size):
        return pl.ds(pl.multiple_of(base * self.height, self.height), size * self.height)

    def send(self, src, dst, axis, bit):
        to = self.partner(axis, bit)
        copy = pltpu.make_async_remote_copy(
            src_ref=src,
            dst_ref=dst,
            send_sem=self.send_sems.at[len(self.copies)],
            recv_sem=self.recv_sems.at[len(self.copies)],
            device_id=(to[CLIP], to[FRAME]),
            device_id_type=MESH,
        )
        copy.start()
        self.copies.append(copy)

    def start(self):
        if self.at < len(self.steps):
            axis, bit = self.steps[self.at]
            mine = self.bit_of(axis, bit)
            half = self.size // 2
            self.send(
                self.held.at[self.rows(self.base + (1 - mine) * half, half)],
                self.slots[self.at],
                axis,
                bit,
            )
            self.base = self.base + mine * half
            self.size = half
        elif self.at < len(self.steps) + len(self.gather):
            done = self.at - len(self.steps)
            axis, bit = self.gather[done]
            size = 1 << done
            region = self.rows((self.slot_of_me // size) * size, size)
            self.send(self.result.at[region], self.result.at[region], axis, bit)

    def advance(self):
        self.copies[self.at].wait_recv()
        if self.at < len(self.steps):
            slot = self.slots[self.at]
            last = self.at == len(self.steps) - 1
            target = self.result if last else self.held
            target_base = self.slot_of_me if last else self.base
            base, held = self.base, self.held

            def add(i, _):
                total = held[self.rows(base + i, 1)].astype(F32) + slot[self.rows(i, 1)].astype(F32)
                target[self.rows(target_base + i, 1)] = total.astype(BF16)
                return 0

            lax.fori_loop(0, self.size, add, 0)
        self.at += 1
        self.start()

    def done(self):
        return self.at == len(self.steps) + len(self.gather)

    def finish(self):
        assert self.done()
        for copy in self.copies:
            copy.wait_send()


def layer_kernel(plan, refs):
    D, T, S, L, FF, nj = plan.D, plan.T, plan.S, plan.L, plan.FF, plan.nj
    me = {CLIP: lax.axis_index(CLIP), FRAME: lax.axis_index(FRAME)}
    frame = me[FRAME]
    xin, gin, n1, qkv, prob, mixed = refs.xin, refs.gin, refs.n1, refs.qkv, refs.prob, refs.mixed
    mid, n2, act, slope, obuf, acc = refs.mid, refs.n2, refs.act, refs.slope, refs.obuf, refs.acc
    dmid, sums = refs.dmid, refs.sums
    for source, target in zip(refs.small, refs.small_rows):
        target[...] = source[...].reshape(1, -1)
    ln1_gain, ln1_bias, b_qv, b_out, ln2_gain, ln2_bias, b_up, b_down = refs.small_rows
    wqkv, wout, wup, wdown = refs.wqkv, refs.wout, refs.wup, refs.wdown
    dbranch, dmixed, igbuf = n2, mixed, obuf

    barrier = pltpu.get_barrier_semaphore()
    greeted = [(me[CLIP], lax.rem(frame + i, plan.F)) for i in range(1, plan.F)]
    for axis, bit in plan.gather_steps():
        flipped = me[axis] + bit * (1 - 2 * ((me[axis] // bit) % 2))
        greeted.append((flipped, frame))
    for peer in greeted:
        pl.semaphore_signal(barrier, inc=1, device_id=peer, device_id_type=MESH)
    pl.semaphore_wait(barrier, len(greeted))

    def tubes(n, device):
        clip_set, tube = n // plan.td, n % plan.td
        return clip_set, ds((device * plan.td + tube) * plan.pos, plan.pos)

    sends = []

    def to_tubes(which, source, target, n):
        arriving = []
        for i in range(plan.F):
            peer = lax.rem(frame + i, plan.F)
            clip_set, positions = tubes(n, peer)
            src = source.at[:, clip_set, positions]
            dst = target.at[n, pl.ds(frame * plan.fd, plan.fd)]
            recv = refs.a2a_recv.at[which, n, i]
            if i == 0:
                copy = pltpu.make_async_copy(src, dst, recv)
                copy.start()
                arriving.append(copy.wait)
            else:
                copy = pltpu.make_async_remote_copy(
                    src_ref=src,
                    dst_ref=dst,
                    send_sem=refs.a2a_send.at[which, n, i],
                    recv_sem=recv,
                    device_id=(me[CLIP], peer),
                    device_id_type=MESH,
                )
                copy.start()
                sends.append(copy.wait_send)
                arriving.append(copy.wait_recv)
        return arriving

    def to_frames(which, source, target, n):
        arriving = []
        for i in range(plan.F):
            peer = lax.rem(frame + i, plan.F)
            clip_set, positions = tubes(n, frame)
            src = source.at[n, pl.ds(peer * plan.fd, plan.fd)]
            dst = target.at[:, clip_set, positions]
            recv = refs.a2a_recv.at[which, n, i]
            if i == 0:
                copy = pltpu.make_async_copy(src, dst, recv)
                copy.start()
                arriving.append((lambda: None, copy.wait))
            else:
                copy = pltpu.make_async_remote_copy(
                    src_ref=src,
                    dst_ref=dst,
                    send_sem=refs.a2a_send.at[which, n, i],
                    recv_sem=recv,
                    device_id=(me[CLIP], peer),
                    device_id_type=MESH,
                )
                copy.start()
                arriving.append((copy.wait_recv, copy.wait_send))
        return arriving

    def wait_all(waits):
        for wait in waits:
            wait()

    x_arrives = [to_tubes(0, refs.stream, xin, 0)]
    g_arrives = []

    loads = []
    for i, (src, dst) in enumerate(zip(refs.from_hbm, (wqkv, wout, wup, wdown))):
        load = pltpu.make_async_copy(src, dst, refs.load_sems.at[i])
        load.start()
        loads.append(load)

    raw = n2
    grad_loads = []
    for r in range(plan.rows):
        grad_load = pltpu.make_async_copy(
            refs.grad.at[r // plan.cd, r % plan.cd],
            raw.at[pl.ds(r * plan.spatial, plan.spatial)],
            refs.grad_sems.at[r],
        )
        grad_load.start()
        grad_loads.append(grad_load.wait)
    wait_all(grad_loads)
    places = (plan.spatial, plan.spatial)
    diagonal = lax.broadcasted_iota(jnp.int32, places, 0) == lax.broadcasted_iota(
        jnp.int32, places, 1
    )
    for r in range(plan.rows):
        kept = refs.mask[pl.ds(r, 1), :] == 1
        keep = jnp.where(diagonal & kept, 1.0, 0.0).astype(BF16)
        rows = dot_nn(keep, raw[pl.ds(r * plan.spatial, plan.spatial), :])
        refs.gsrc[r // plan.cd, r % plan.cd] = rows.astype(BF16)
    for n in range(1, S):
        wait_all(sends)
        sends.clear()
        x_arrives.append(to_tubes(0, refs.stream, xin, n))

    scatters = [
        Scatter(
            plan,
            me,
            part,
            refs.groups[group],
            refs.group_slots[group],
            refs.res.at[group],
            refs.rs_send,
            refs.rs_recv,
        )
        for part, (group, *_) in enumerate(plan.parts)
    ]

    def start(group):
        for part, scatter in enumerate(scatters):
            if plan.parts[part][0] == group:
                scatter.start()

    def tick(name):
        for part in DUE.get(name, ()):
            if part < len(scatters) and scatters[part].copies and not scatters[part].done():
                scatters[part].advance()

    def pieces(name, count, total, body):
        for i in range(count):
            lax.fori_loop(total * i // count, total * (i + 1) // count, body, 0)
            tick(name + str(i))

    def seq_rows(ref, s, start, size):
        frames = size // plan.pos
        block = ref[s, pl.ds(start // plan.pos, frames)]
        return block.reshape(size, D)

    sums[...] = jnp.zeros_like(sums)

    def tally(i, value):
        sums[i] += fold8(value)

    lanes = lax.broadcasted_iota(jnp.int32, (1, 128), 1)
    head_masks = [(lanes < 64).astype(BF16), (lanes >= 64).astype(BF16)]
    scale = 1.0 / math.sqrt(D // HEADS)

    def head_columns(pair):
        at = pair * 128
        return tuple(ds(first + at, 128) for first in (0, 0, D, 2 * D))

    for s in range(S):
        wait_all(x_arrives[s])
        if s == S - 1:
            g_arrives += [to_tubes(1, refs.gsrc, gin, n) for n in range(S)]

        def first_norm(i, _):
            x = seq_rows(xin, s, i * ROW_BLOCK, ROW_BLOCK).astype(F32)
            unit, _ = unit_norm(x)
            tally(8, x * x)
            n1[ds(s * L + i * ROW_BLOCK, ROW_BLOCK), :] = (unit * ln1_gain[...] + ln1_bias[...]).astype(BF16)
            return 0

        lax.fori_loop(0, L // ROW_BLOCK, first_norm, 0)
        if s == 0:
            loads[0].wait()
        tokens = pl.ds(s * L, L)
        for third in range(3):
            columns = pl.ds(third * D, D)
            out = dot_nn(n1[tokens, :], wqkv[:, columns])
            if third != 1:
                out = out + b_qv[:, pl.ds(third // 2 * D, D)]
            if third == 0:
                out = out * scale
            qkv[tokens, columns] = out.astype(BF16)

        def attend(pair, _):
            columns, q_at, k_at, v_at = head_columns(pair)
            q, k, v = qkv[tokens, q_at], qkv[tokens, k_at], qkv[tokens, v_at]
            out = jnp.zeros((L, 128), F32)
            for e in range(2):
                scores = dot_nt(q * head_masks[e], k)
                power = jnp.exp(scores - jnp.max(scores, axis=-1, keepdims=True))
                share = 1.0 / jnp.sum(power, axis=-1, keepdims=True)
                weight = (power * share).astype(BF16)
                prob[s * HEADS + pair * 2 + e] = weight
                out = out + dot_nn(weight, v * head_masks[e])
            mixed[tokens, columns] = out.astype(BF16)
            return 0

        lax.fori_loop(0, HEADS // 2, attend, 0)

    loads[1].wait()

    mid[...] = dot_nn(mixed[...], wout[...]) + b_out[...]
    for s in range(S):

        def second_norm(i, _):
            rows = ds(s * L + i * ROW_BLOCK, ROW_BLOCK)
            branch = mid[rows, :]
            middle = seq_rows(xin, s, i * ROW_BLOCK, ROW_BLOCK).astype(F32) + branch
            mid[rows, :] = middle
            tally(9, middle * middle)
            tally(11, branch * branch)
            unit, _ = unit_norm(middle)
            n2[rows, :] = (unit * ln2_gain[...] + ln2_bias[...]).astype(BF16)
            return 0

        lax.fori_loop(0, L // ROW_BLOCK, second_norm, 0)

    loads[2].wait()

    def up(i, _):
        columns = ds(i * D, D)
        hidden = dot_nn(n2[...], wup[:, columns]) + b_up[:, columns]
        active, steep = gelu_and_slope(hidden)
        act[:, columns] = active.astype(BF16)
        slope[:, columns] = steep.astype(BF16)
        return 0

    lax.fori_loop(0, nj, up, 0)
    loads[3].wait()
    out_arrives = []
    for s in range(S):
        tokens = pl.ds(s * L, L)
        branch = dot_nn(act[tokens, :], wdown[...]) + b_down[...]
        result = branch + mid[tokens, :]
        tally(10, result * result)
        tally(12, branch * branch)
        obuf[s] = result.astype(BF16).reshape(FRAMES, plan.pos, D)
        out_arrives += to_frames(2, obuf, refs.out_h, s)

    for s in range(S):
        wait_all(g_arrives[s])
    wait_all(sends)
    sends.clear()
    def put(group, chunk, frame_block, block):
        for of_group, order, first, height in plan.parts:
            if of_group == group:
                at = plan.place(order, chunk, frame_block)
                rows = pl.multiple_of(first * plan.blocks + at * height, 16)
                piece = block[first : first + height]
                refs.groups[group][pl.ds(rows, height), :] = piece.astype(BF16)

    def grad_down(i, _):
        out = dot_tn(act[:, ds(i * D, D)], gin[...].reshape(T, D))
        share = FF // plan.F
        for n in range(D // plan.R):
            place = n * plan.R
            frames = D // share
            chunk = place % share // plan.R
            put(0, chunk, i * frames + place // share, out[place : place + plan.R])
        return 0

    pieces("GD", nj, nj, grad_down)
    start(0)

    def through_gelu(i, _):
        columns = ds(i * D, D)
        d_active = dot_nt(gin[...].reshape(T, D), wdown[columns, :])
        d_hidden = (d_active * slope[:, columns].astype(F32)).astype(BF16)
        slope[:, columns] = d_hidden
        sums[13 + i] += fold8(d_hidden.astype(F32))
        return 0

    pieces("TG", nj, nj, through_gelu)

    def grad_columns(group, chunk, lhs, rhs):
        out = dot_tn(lhs, rhs)
        for f in range(plan.F):
            put(group, chunk, f, out[f * plan.R : (f + 1) * plan.R])

    def grad_up(c, _):
        grad_columns(1, c, n2[...], slope[:, ds(c * D, D)])
        return 0

    pieces("GU", plan.C, plan.C, grad_up)
    start(1)
    acc[...] = dot_nt(slope[...], wup[...])
    tick("DT")

    for s in range(S):

        def second_norm_back(i, _):
            rows = ds(s * L + i * ROW_BLOCK, ROW_BLOCK)
            up_grad = acc[rows, :]
            unit, inverse = unit_norm(mid[rows, :])
            g = seq_rows(gin, s, i * ROW_BLOCK, ROW_BLOCK).astype(F32)
            d_middle = g + norm_pull(up_grad * ln2_gain[...], unit, inverse)
            dmid[rows, :] = d_middle
            low = d_middle.astype(BF16)
            dbranch[rows, :] = low
            tally(4, low.astype(F32))
            tally(5, up_grad * unit)
            tally(6, up_grad)
            tally(7, g)
            return 0

        lax.fori_loop(0, L // ROW_BLOCK, second_norm_back, 0)
        tick("LB" + str(s))

    grad_columns(2, plan.C - 1, mixed[...], dbranch[...])
    tick("DO")
    dmixed[...] = dot_nt(dbranch[...], wout[...]).astype(BF16)
    tick("DM")

    for s in range(S):
        tokens = pl.ds(s * L, L)

        def attend_back(pair, _):
            columns, q_at, k_at, v_at = head_columns(pair)
            q, k, v = qkv[tokens, q_at], qkv[tokens, k_at], qkv[tokens, v_at]
            d_out = dmixed[tokens, columns]
            zero = jnp.zeros((L, 128), F32)
            d_q, d_k, d_v = zero, zero, zero
            for e in range(2):
                weight = prob[s * HEADS + pair * 2 + e]
                own = d_out * head_masks[e]
                d_weight = dot_nt(own, v)
                d_v = d_v + dot_tn(weight, own)
                wide_weight = weight.astype(F32)
                centre = jnp.sum(wide_weight * d_weight, axis=-1, keepdims=True)
                d_score = (wide_weight * (d_weight - centre)).astype(BF16)
                d_q = d_q + dot_nn(d_score, k * head_masks[e])
                d_k = d_k + dot_tn(d_score, q * head_masks[e])
            qkv[tokens, q_at] = (d_q * scale).astype(BF16)
            qkv[tokens, k_at] = d_k.astype(BF16)
            qkv[tokens, v_at] = d_v.astype(BF16)
            return 0

        pieces("AB" + str(s), 2, HEADS // 2, attend_back)

    def grad_qkv(c, _):
        grad_columns(2, c, n1[...], qkv[:, ds(c * D, D)])
        return 0

    pieces("GQ", plan.C - 1, plan.C - 1, grad_qkv)
    start(2)
    acc[...] = dot_nt(qkv[...], wqkv[...])
    tick("D1")
    for recv, send in out_arrives:
        send()
    in_arrives = []
    for s in range(S):

        def first_norm_back(i, _):
            rows = ds(s * L + i * ROW_BLOCK, ROW_BLOCK)
            up_grad = acc[rows, :]
            x = seq_rows(xin, s, i * ROW_BLOCK, ROW_BLOCK).astype(F32)
            unit, inverse = unit_norm(x)
            total = dmid[rows, :] + norm_pull(up_grad * ln1_gain[...], unit, inverse)
            frames = ROW_BLOCK // plan.pos
            igbuf[s, pl.ds(i * frames, frames)] = total.astype(BF16).reshape(frames, plan.pos, D)
            tally(0, up_grad * unit)
            tally(1, up_grad)
            tally(2, qkv[rows, pl.ds(0, D)].astype(F32))
            tally(3, qkv[rows, pl.ds(2 * D, D)].astype(F32))
            return 0

        lax.fori_loop(0, L // ROW_BLOCK, first_norm_back, 0)
        in_arrives += to_frames(3, igbuf, refs.ig_h, s)
        tick("L1" + str(s))

    vbuf, vrecv = refs.vbuf, refs.vrecv
    count = sums.shape[0]
    for i in range(count):
        vbuf[0, pl.ds(i, 1), :] = jnp.sum(sums[i], axis=0, keepdims=True)
    hops = plan.steps("xyz")
    small = []
    for i, (axis, bit) in enumerate(hops):
        flipped = me[axis] + bit * (1 - 2 * ((me[axis] // bit) % 2))
        to = {**me, axis: flipped}
        copy = pltpu.make_async_remote_copy(
            src_ref=vbuf.at[i],
            dst_ref=vrecv.at[i],
            send_sem=refs.v_send.at[i],
            recv_sem=refs.v_recv.at[i],
            device_id=(to[CLIP], to[FRAME]),
            device_id_type=MESH,
        )
        copy.start()
        small.append(copy)
        tick("V" + str(i))
        copy.wait_recv()
        vbuf[i + 1] = vbuf[i] + vrecv[i]
    refs.vec[...] = vbuf[len(hops)]
    for copy in small:
        copy.wait_send()
    tick("END")
    while not all(scatter.done() for scatter in scatters):
        for scatter in scatters:
            if not scatter.done():
                scatter.advance()
    for scatter in scatters:
        scatter.finish()
    for recv, send in out_arrives:
        recv()
    for recv, send in in_arrives:
        send()
        recv()
    wait_all(sends)


def fused(plan, stream, out_grad, token_mask, weights, small):
    D, T, S, L, FF = plan.D, plan.T, plan.S, plan.L, plan.FF
    n_steps = len(plan.steps("xyz"))
    n_parts = len(plan.parts)
    n_hops = n_steps + len(plan.gather_steps())
    n_vec = 13 + plan.nj
    vec_rows = -(-n_vec // 8) * 8
    vmem = lambda shape, kind=BF16: pltpu.VMEM(shape, kind)
    token_shape = (plan.fd, plan.cd, plan.spatial, D)
    scratch = dict(
        wqkv=vmem((D, 3 * D)),
        wout=vmem((D, D)),
        wup=vmem((D, FF)),
        wdown=vmem((FF, D)),
        xin=vmem((S, FRAMES, plan.pos, D)),
        gin=vmem((S, FRAMES, plan.pos, D)),
        n1=vmem((T, D)),
        qkv=vmem((T, 3 * D)),
        prob=vmem((S * HEADS, L, L)),
        mixed=vmem((T, D)),
        mid=vmem((T, D), F32),
        n2=vmem((T, D)),
        act=vmem((T, FF)),
        slope=vmem((T, FF)),
        obuf=vmem((S, FRAMES, plan.pos, D)),
        acc=vmem((T, D), F32),
        dmid=vmem((T, D), F32),
        sums=vmem((n_vec, 8, D), F32),
        g_down=vmem((plan.whole, D)),
        g_up=vmem((plan.whole, D)),
        vbuf=vmem((n_steps + 1, vec_rows, D), F32),
        vrecv=vmem((n_steps, vec_rows, D), F32),
        small_rows=[vmem((1, item.size), F32) for item in small],
        gsrc=vmem(token_shape),
        load_sems=pltpu.SemaphoreType.DMA((4,)),
        grad_sems=pltpu.SemaphoreType.DMA((plan.rows,)),
        a2a_send=pltpu.SemaphoreType.DMA((4, S, plan.F)),
        a2a_recv=pltpu.SemaphoreType.DMA((4, S, plan.F)),
        rs_send=pltpu.SemaphoreType.DMA((n_parts, n_hops)),
        rs_recv=pltpu.SemaphoreType.DMA((n_parts, n_hops)),
        v_send=pltpu.SemaphoreType.DMA((n_steps,)),
        v_recv=pltpu.SemaphoreType.DMA((n_steps,)),
        slots=[
            vmem((3, plan.whole >> (i + 1), D)) for i in range(n_steps)
        ],
    )

    def kernel(stream, grad, wqkv, wout, wup, wdown, mask, *rest):
        count = len(small)
        refs = SimpleNamespace(
            stream=stream,
            grad=grad,
            from_hbm=(wqkv, wout, wup, wdown),
            mask=mask,
            small=rest[:count],
        )
        refs.out_h, refs.ig_h, refs.res, refs.vec = rest[count : count + 4]
        vars(refs).update(rest[count + 4])
        refs.groups = (refs.g_down, refs.g_up, refs.wdown)
        refs.group_slots = [[slot.at[group] for slot in refs.slots] for group in range(3)]
        layer_kernel(plan, refs)

    hbm = pl.BlockSpec(memory_space=pl.ANY)
    in_vmem = pl.BlockSpec(memory_space=pltpu.VMEM)
    return pl.pallas_call(
        kernel,
        out_shape=(
            jax.ShapeDtypeStruct(token_shape, BF16),
            jax.ShapeDtypeStruct(token_shape, BF16),
            jax.ShapeDtypeStruct((3, plan.C * plan.R, D), BF16),
            jax.ShapeDtypeStruct((vec_rows, D), F32),
        ),
        in_specs=[hbm] * 6 + [in_vmem] * (1 + len(small)),
        out_specs=(hbm, hbm, in_vmem, in_vmem),
        scratch_shapes=(scratch,),
        compiler_params=pltpu.CompilerParams(
            collective_id=0, has_side_effects=True, vmem_limit_bytes=VMEM_LIMIT
        ),
        name="tube_layer",
    )(
        stream.reshape(token_shape),
        out_grad.reshape(token_shape),
        *weights,
        token_mask,
        *small,
    )


VMEM_LIMIT = 64 * 1024 * 1024 - 512 * 1024


def finish_kernel(plan, out_s, ig_s, res_h, vec_h, out_d, ig_d, *refs):
    C, R, D = plan.C, plan.R, plan.D
    qkv_d, up_d, proj_d, down_d = refs[:4]
    vectors, statistics = refs[4:12], refs[12]
    qkv_v, up_v, proj_v, down_v, res, vec, out_v, ig_v, sems = refs[13:]
    moves = [(res_h.at[group], res.at[group]) for group in range(3)]
    moves += [(vec_h, vec), (out_s, out_v), (ig_s, ig_v)]
    copies = [pltpu.make_async_copy(*move, sems.at[i]) for i, move in enumerate(moves)]
    for copy in copies:
        copy.start()

    def write(value, target):
        copy = pltpu.make_async_copy(value, target, sems.at[len(copies)])
        copy.start()
        copies.append(copy)

    def each_piece(group):
        for of_group, _, first, height in plan.parts:
            if of_group == group:
                for chunk in range(C):
                    block = res[group, pl.ds(first * C + chunk * height, height), :]
                    yield chunk, first, height, block.astype(F32)

    copies[0].wait()
    for chunk, first, height, block in each_piece(0):
        down_v[pl.ds(chunk * R + first, height), :] = block
    write(down_v, down_d)
    copies[1].wait()
    for chunk, first, height, block in each_piece(1):
        up_v[pl.ds(first, height), pl.ds(chunk * D, D)] = block
    write(up_v, up_d)
    copies[2].wait()
    for chunk, first, height, block in each_piece(2):
        if chunk < C - 1:
            qkv_v[pl.ds(first, height), pl.ds(chunk * D, D)] = block
        else:
            proj_v[pl.ds(first, height), :] = block
    write(qkv_v, qkv_d)
    write(proj_v, proj_d)
    copies[4].wait()
    write(out_v, out_d)
    copies[5].wait()
    write(ig_v, ig_d)

    copies[3].wait()
    frame = lax.axis_index(FRAME)
    counts = (1, 1, 2, 1, 1, 1, plan.nj, 1)
    firsts = (0, 1, 2, 4, 5, 6, 13, 7)
    for target, count, first in zip(vectors, counts, firsts):
        share = count * D // plan.F
        per_row = plan.F // count
        row = vec[pl.ds(first + frame // per_row, 1), :]
        turned = pltpu.roll(row, lax.rem(D - (frame % per_row) * share, D), 1)
        target[...] = turned[:, :share].reshape(-1)
    squares = jnp.sum(vec[pl.ds(8, 8), :], axis=-1, keepdims=True)
    entries = plan.T * D * C * plan.F
    roots = jnp.sqrt(squares / entries)
    lanes = lax.broadcasted_iota(jnp.int32, (8, 8), 1)
    rows = lax.broadcasted_iota(jnp.int32, (8, 8), 0)
    across = jnp.sum(jnp.where(lanes == rows, roots, 0.0), axis=0, keepdims=True)
    statistics[...] = across[:, :5].reshape(-1)
    for copy in copies[6:]:
        copy.wait()


def finish(plan, output, input_grad, res, vec):
    D, F, C, R = plan.D, plan.F, plan.C, plan.R
    shapes = [(R, 3 * D), (R, C * D), (R, D), (C * R, D)]
    vectors = [(count * D // F,) for count in (1, 1, 2, 1, 1, 1, plan.nj, 1)]
    hbm = pl.BlockSpec(memory_space=pltpu.HBM)
    in_vmem = pl.BlockSpec(memory_space=pltpu.VMEM)
    like = lambda item: jax.ShapeDtypeStruct(item.shape, item.dtype)
    return pl.pallas_call(
        functools.partial(finish_kernel, plan),
        out_shape=tuple(
            [like(output), like(input_grad)]
            + [jax.ShapeDtypeStruct(shape, F32) for shape in shapes + vectors + [(5,)]]
        ),
        in_specs=[hbm] * 4,
        out_specs=tuple([hbm] * 6 + [in_vmem] * 9),
        scratch_shapes=[pltpu.VMEM(shape, F32) for shape in shapes]
        + [pltpu.VMEM(res.shape, BF16), pltpu.VMEM(vec.shape, F32)]
        + [pltpu.VMEM(output.shape, BF16)] * 2
        + [pltpu.SemaphoreType.DMA((12,))],
        compiler_params=pltpu.CompilerParams(vmem_limit_bytes=VMEM_LIMIT),
        name="tube_layer_results",
    )(output, input_grad, res, vec)


def with_kernel(
    plan,
    stream,
    out_grad,
    token_mask,
    ln1_gain,
    ln1_bias,
    w_qkv,
    b_qv,
    w_out,
    b_out,
    ln2_gain,
    ln2_bias,
    w_up,
    b_up,
    w_down,
    b_down,
):
    small = (ln1_gain, ln1_bias, b_qv, b_out, ln2_gain, ln2_bias, b_up, b_down)
    parts = fused(plan, stream, out_grad, token_mask, (w_qkv, w_out, w_up, w_down), small)
    output, input_grad, g_qkv, g_up, g_out, g_down, *vectors, statistics = finish(plan, *parts)
    return (
        output.reshape(stream.shape),
        input_grad.reshape(stream.shape),
        vectors[0],
        vectors[1],
        g_qkv,
        vectors[2],
        g_out,
        vectors[3],
        vectors[4],
        vectors[5],
        g_up,
        vectors[6],
        g_down,
        vectors[7],
        statistics,
    )


def layer_norm(inputs, norm_gain, norm_shift):
    center = jnp.mean(inputs, axis=-1, keepdims=True)
    shifted = inputs - center
    spread = jnp.mean(shifted * shifted, axis=-1, keepdims=True)
    inverse = lax.rsqrt(spread + EPS)
    unit = shifted * inverse
    return (unit * norm_gain + norm_shift, unit, inverse)


def norm_backward(upstream, unit, inverse, norm_gain):
    scaled = upstream * norm_gain
    first = jnp.mean(scaled, axis=-1, keepdims=True)
    second = jnp.mean(scaled * unit, axis=-1, keepdims=True)
    return inverse * (scaled - first - unit * second)


def gelu_slope(hidden_state):
    cumulative = 0.5 * (1.0 + lax.erf(hidden_state * (1.0 / math.sqrt(2.0))))
    density = jnp.exp(-0.5 * hidden_state * hidden_state) * (1.0 / math.sqrt(2.0 * math.pi))
    return cumulative + hidden_state * density


def with_collectives(
    stream,
    out_grad,
    token_mask,
    ln1_gain,
    ln1_bias,
    w_qkv,
    b_qv,
    w_out,
    b_out,
    ln2_gain,
    ln2_bias,
    w_up,
    b_up,
    w_down,
    b_down,
):
    frame_count = lax.axis_size(FRAME)
    clip_count = lax.axis_size(CLIP)
    device_count = clip_count * frame_count
    frame_split = min(FRAMES, frame_count)
    clip_split = frame_count // frame_split
    frames_dev = FRAMES // frame_split
    tubes_dev = TUBES // frame_split
    row_count, spatial, width = stream.shape
    clips_dev = row_count // frames_dev
    clip_sets = clips_dev // clip_split
    tube_pos = spatial // TUBES
    length = FRAMES * tube_pos
    head_dim = width // HEADS
    scale = 1.0 / math.sqrt(head_dim)

    def leaving(tensor):
        return tensor.reshape(frames_dev, clip_sets, frame_count, tubes_dev * tube_pos, width)

    def arranged(tensor):
        tensor = tensor.reshape(clip_split, FRAMES, clip_sets, tubes_dev, tube_pos, width)
        tensor = jnp.transpose(tensor, (0, 2, 3, 1, 4, 5))
        return tensor.reshape(-1, width)

    def restored(tensor):
        tensor = tensor.reshape(clip_split, clip_sets, tubes_dev, FRAMES, tube_pos, width)
        tensor = jnp.transpose(tensor, (0, 3, 1, 2, 4, 5))
        return tensor.reshape(frame_count * frames_dev, clip_sets, 1, tubes_dev * tube_pos, width)

    masked = jnp.where(token_mask[:, :, None] == 1, out_grad, jnp.zeros((), jnp.bfloat16))
    arrived = (
        lax.all_to_all(leaving(stream), FRAME, split_axis=2, concat_axis=0, tiled=True),
        lax.all_to_all(leaving(masked), FRAME, split_axis=2, concat_axis=0, tiled=True),
    )
    inputs = arranged(arrived[0]).astype(jnp.float32)
    grad_y = arranged(arrived[1])
    seq_count = inputs.shape[0] // length

    def split_heads(tensor):
        return tensor.reshape(seq_count, length, HEADS, head_dim)

    def attention_scores(queries, key_part):
        return (
            jnp.einsum("slhe,smhe->shlm", queries, key_part, preferred_element_type=jnp.float32)
            * scale
        )

    first_normed_input, unit_one, inverse_one = layer_norm(inputs, ln1_gain, ln1_bias)
    first_normed_input = first_normed_input.astype(jnp.bfloat16)
    third_bias_term = jnp.concatenate(
        [b_qv[:width], jnp.zeros((width,), jnp.float32), b_qv[width:]]
    )
    query_key_value = (
        jnp.dot(first_normed_input, w_qkv, preferred_element_type=jnp.float32) + third_bias_term
    ).astype(jnp.bfloat16)
    queries = split_heads(query_key_value[:, :width])
    key_part = split_heads(query_key_value[:, width : 2 * width])
    values = split_heads(query_key_value[:, 2 * width :])
    scores = attention_scores(queries, key_part)
    largest = jnp.max(scores, axis=-1, keepdims=True)
    logsum = largest + jnp.log(jnp.sum(jnp.exp(scores - largest), axis=-1, keepdims=True))
    attend_low = jnp.exp(scores - logsum).astype(jnp.bfloat16)
    mixed_heads = jnp.einsum(
        "shlm,smhe->slhe", attend_low, values, preferred_element_type=jnp.float32
    )
    mixed_heads = mixed_heads.reshape(-1, width).astype(jnp.bfloat16)
    attention_branch = jnp.dot(mixed_heads, w_out, preferred_element_type=jnp.float32) + b_out
    middle = inputs + attention_branch
    second_normed_input, unit_two, inverse_two = layer_norm(middle, ln2_gain, ln2_bias)
    second_normed_input = second_normed_input.astype(jnp.bfloat16)
    hidden_state = jnp.dot(second_normed_input, w_up, preferred_element_type=jnp.float32) + b_up
    activated_hidden = jax.nn.gelu(hidden_state, approximate=False).astype(jnp.bfloat16)
    feedforward_branch = (
        jnp.dot(activated_hidden, w_down, preferred_element_type=jnp.float32) + b_down
    )
    result = middle + feedforward_branch
    squares = jnp.stack(
        [
            jnp.sum(inputs * inputs),
            jnp.sum(middle * middle),
            jnp.sum(result * result),
            jnp.sum(attention_branch * attention_branch),
            jnp.sum(feedforward_branch * feedforward_branch),
        ]
    )
    totals = lax.psum(squares, (CLIP, FRAME))
    statistics = jnp.sqrt(totals / (row_count * spatial * width * device_count))
    grad_w_down = jnp.einsum(
        "tf,td->fd", activated_hidden, grad_y, preferred_element_type=jnp.float32
    )
    grad_b_down = jnp.sum(grad_y.astype(jnp.float32), axis=0)
    d_active = jnp.einsum("td,fd->tf", grad_y, w_down, preferred_element_type=jnp.float32)
    d_hidden = (d_active * gelu_slope(hidden_state)).astype(jnp.bfloat16)
    grad_w_up = jnp.einsum(
        "td,tf->df", second_normed_input, d_hidden, preferred_element_type=jnp.float32
    )
    grad_b_up = jnp.sum(d_hidden.astype(jnp.float32), axis=0)
    d_two = jnp.einsum("tf,df->td", d_hidden, w_up, preferred_element_type=jnp.float32)
    grad_ln2_gain = jnp.sum(d_two * unit_two, axis=0)
    grad_ln2_bias = jnp.sum(d_two, axis=0)
    d_middle = grad_y.astype(jnp.float32) + norm_backward(d_two, unit_two, inverse_two, ln2_gain)
    d_branch = d_middle.astype(jnp.bfloat16)
    grad_w_out = jnp.einsum("td,te->de", mixed_heads, d_branch, preferred_element_type=jnp.float32)
    grad_b_out = jnp.sum(d_branch.astype(jnp.float32), axis=0)
    d_mixed = jnp.einsum("te,de->td", d_branch, w_out, preferred_element_type=jnp.float32)
    d_mixed = split_heads(d_mixed.astype(jnp.bfloat16))
    again = attention_scores(queries, key_part)
    attend = jnp.exp(again - logsum)
    attend_again = attend.astype(jnp.bfloat16)
    d_attend = jnp.einsum("slhe,smhe->shlm", d_mixed, values, preferred_element_type=jnp.float32)
    d_values = jnp.einsum(
        "shlm,slhe->smhe", attend_again, d_mixed, preferred_element_type=jnp.float32
    )
    centre_term = jnp.sum(attend * d_attend, axis=-1, keepdims=True)
    d_scores = (attend * (d_attend - centre_term)).astype(jnp.bfloat16)
    d_queries = (
        jnp.einsum("shlm,smhe->slhe", d_scores, key_part, preferred_element_type=jnp.float32)
        * scale
    )
    d_keys = (
        jnp.einsum("shlm,slhe->smhe", d_scores, queries, preferred_element_type=jnp.float32) * scale
    )
    d_qkv = jnp.concatenate(
        [d_queries.reshape(-1, width), d_keys.reshape(-1, width), d_values.reshape(-1, width)],
        axis=1,
    ).astype(jnp.bfloat16)
    grad_w_qkv = jnp.einsum(
        "td,te->de", first_normed_input, d_qkv, preferred_element_type=jnp.float32
    )
    bias_sums = jnp.sum(d_qkv.astype(jnp.float32), axis=0)
    grad_b_qv = jnp.concatenate([bias_sums[:width], bias_sums[2 * width :]])
    d_one = jnp.einsum("te,de->td", d_qkv, w_qkv, preferred_element_type=jnp.float32)
    grad_ln1_gain = jnp.sum(d_one * unit_one, axis=0)
    grad_ln1_bias = jnp.sum(d_one, axis=0)
    d_inputs = d_middle + norm_backward(d_one, unit_one, inverse_one, ln1_gain)
    departed = (
        lax.all_to_all(
            restored(result.astype(jnp.bfloat16)), FRAME, split_axis=0, concat_axis=2, tiled=True
        ),
        lax.all_to_all(
            restored(d_inputs.astype(jnp.bfloat16)),
            FRAME,
            split_axis=0,
            concat_axis=2,
            tiled=True,
        ),
    )
    output = departed[0].reshape(row_count, spatial, width)
    input_grad = departed[1].reshape(row_count, spatial, width)
    gradients = [
        grad_ln1_gain,
        grad_ln1_bias,
        grad_w_qkv,
        grad_b_qv,
        grad_w_out,
        grad_b_out,
        grad_ln2_gain,
        grad_ln2_bias,
        grad_w_up,
        grad_b_up,
        grad_w_down,
        grad_b_down,
    ]
    grouped = jnp.concatenate([item.reshape(frame_count, -1) for item in gradients], axis=1)
    extent_all = grouped.shape[1]
    padding = -extent_all % clip_count
    grouped = jnp.concatenate([grouped, jnp.zeros((frame_count, padding), jnp.float32)], axis=1)
    own_rows = lax.psum_scatter(
        grouped.astype(jnp.bfloat16), FRAME, scatter_dimension=0, tiled=True
    ).astype(jnp.float32)
    summed = lax.psum(own_rows, CLIP).reshape(-1)
    finished = []
    offset = 0
    for item in gradients:
        extent = item.size // frame_count
        local_shape = (item.shape[0] // frame_count,) + item.shape[1:]
        finished.append(summed[offset : offset + extent].reshape(local_shape))
        offset = offset + extent
    return (
        output,
        input_grad,
        finished[0],
        finished[1],
        finished[2],
        finished[3],
        finished[4],
        finished[5],
        finished[6],
        finished[7],
        finished[8],
        finished[9],
        finished[10],
        finished[11],
        statistics,
    )


def solution(mesh):
    clips, frames = mesh.shape[CLIP], mesh.shape[FRAME]

    def on_device(stream, *rest):
        ff = rest[-4].shape[1]
        plan = Plan(clips, frames, stream.shape, ff)
        if plan.fits:
            return with_kernel(plan, stream, *rest)
        return with_collectives(stream, *rest)

    tokens = P((CLIP, FRAME), None, None)
    in_specs = (tokens, tokens, P((CLIP, FRAME), None)) + (P(),) * 12
    rows, vector = P(FRAME, None), P(FRAME)
    out_specs = (
        tokens,
        tokens,
        vector,
        vector,
        rows,
        vector,
        rows,
        vector,
        vector,
        vector,
        rows,
        vector,
        rows,
        vector,
        P(),
    )
    return jax.shard_map(
        on_device, mesh=mesh, in_specs=in_specs, out_specs=out_specs, check_vma=False
    )
```

time: 218 us -> 141 us (0.65)
  Pallas kernels: 191 us -> 139 us
  local copies, waits for them, and re-layouts: 21.6 us -> 0 us
  other arithmetic: 4.22 us -> 0 us
    pallas_call x1, Pallas kernels: 191 us -> 135 us  [fused(): pl.pallas_call(kernel, out_shape=(jax.ShapeDtypeStruct(token_shape, BF16)...]
    unnamed x16 -> x0, local copies, waits for them, and re-layouts: 9.96 us -> none
    slice x5 -> x0, local copies, waits for them, and re-layouts: 4.55 us -> none  [the longest x3 2.52 us: own(): flat = totals[first:first + count].reshape(-1)]
    pallas_call x0 -> x1, Pallas kernels: none -> 4.15 us  [finish(): pl.pallas_call(functools.partial(finish_kernel, plan), out_shape=tuple([l...]
    dynamic_slice x5 -> x0, local copies, waits for them, and re-layouts: 3.06 us -> none  [own(): return lax.dynamic_slice(flat, (frame * share,), (share,))]
where the time goes in v2:
time: 141 us; the launch traced here: 140 us
  Pallas kernels  139 us (99%)
    pallas_call x1, Pallas kernels, fused(): pl.pallas_call(kernel, out_shape=(jax.ShapeDtypeStruct(token_shape, BF16)...  135 us
    pallas_call x1, Pallas kernels, finish(): pl.pallas_call(functools.partial(finish_kernel, plan), out_shape=tuple([l...  4.15 us

profile of v2, /device:TPU:1, one launch (start us, length us, event | category | flops | bytes accessed | tf_op | source)
XLA Modules:
  0.0 139.6 jit_solution(10663535353755894624)
XLA Ops:
  0.7 134.6 %tube_layer.1 = (bf16[2,1,256,768]{3,2,1,0:T(8,128)(2,1)}, bf16[2,1,256,768]{3,2,1,0:T(8,128)(2,1)}, bf16[3,384,768]{2,1,0:T(8,128)(2,1)}, f32[24,768]{1,0:T(8,128)}) custom-call(bf16[2,1,256,768]{3,2,1,0:T(8,128)(2,1)} %bitcast.4, bf16[2,1,256,768]{3,2,1,0:T(8,128)(2,1)} %bitcast.5, bf16[768,2304]{1,0:T(8,128)(2,1)} %wqkv.1, bf16[768,768]{1,0:T(8,128)(2,1)} %wout.1, ...), custom_call_target="tpu_custom_call" | custom-call | tf_op jit(solution)/shard_map/tube_layer/pallas_call | solution.py:725
  135.3 4.2 %tube_layer_results.1 = (bf16[2,1,256,768]{3,2,1,0:T(8,128)(2,1)}, bf16[2,1,256,768]{3,2,1,0:T(8,128)(2,1)}, f32[96,2304]{1,0:T(8,128)}, f32[96,3072]{1,0:T(8,12...) custom-call(bf16[2,1,256,768]{3,2,1,0:T(8,128)(2,1)} %get-tuple-elem, ...), custom_call_target="tpu_custom_call" | custom-call | tf_op jit(solution)/shard_map/tube_layer_results/pallas_call | solution.py:824

commit v3 on v2

--- a/solution.py
+++ b/solution.py
@@ -24,26 +24,26 @@
 
 SIXTHS = 6
 SHARES = (
-    (("yzx", 2), ("xyz", 2), ("zyx", 2),),
-    (("yxz", 2), ("xzy", 2), ("xyz", 2),),
-    (("xzy", 2), ("yxz", 2), ("xyz", 2),),
+    (("zyx", 2), ("xzy", 1), ("yzx", 1), ("yxz", 2),),
+    (("xzy", 1), ("xyz", 3), ("yxz", 2),),
+    (("xzy", 2), ("xyz", 2), ("yxz", 2),),
 )
 DUE = dict(
-    GU1=(0,),
-    GU2=(1,),
-    GU3=(2,),
-    DM=(3, 4),
-    AB00=(5,),
-    AB01=(0, 1),
-    AB10=(2,),
-    D1=(0, 3, 4),
-    L11=(1,),
-    V0=(6, 7, 8, 2, 5),
-    V1=(0, 4, 3, 6, 1, 7, 2, 8, 5, 0),
-    V2=(3, 4, 8, 7, 6, 2, 0, 1, 4),
-    V3=(0, 5, 2, 1, 2, 3, 4, 1, 8, 4, 3, 7, 3, 6),
-    V4=(5, 6, 8, 7, 5, 6, 5, 8, 6),
-    END=(7, 8, 7),
+    GU0=(0, 1),
+    GU1=(2, 3),
+    DT=(4,),
+    LB1=(5, 6),
+    DO=(1,),
+    AB00=(2,),
+    AB01=(0,),
+    AB10=(4,),
+    AB11=(1,),
+    GQ0=(2, 3),
+    V0=(7, 4, 8, 5, 9, 0, 6, 1),
+    V1=(3, 2, 7, 5, 3, 8, 7, 6, 9, 4, 5, 0, 2, 3, 1),
+    V2=(6, 9, 7, 8, 4, 0, 2, 3, 2, 1, 5, 4, 7, 3),
+    V3=(9, 1, 0, 4, 6, 0, 8, 5, 7, 5, 6, 7),
+    V4=(9, 6, 8, 9, 8, 9, 8),
 )
 
 
@@ -124,7 +124,7 @@
         powers = all(n & (n - 1) == 0 for n in (clips, frames, self.X, self.Y))
         self.fits = (
             self.clip_split == 1
-            and clips >= 2
+            and clips >= 4
             and powers
             and frames % 2 == 0
             and self.R % (16 * SIXTHS) == 0
@@ -141,6 +141,9 @@
             z=[(FRAME, self.Y * b) for b in bits(self.F // self.Y)],
         )
         return [(CLIP, 1)] + along[order[0]] + along[order[1]] + along[order[2]]
+
+    def peer_order(self):
+        return range(self.F - 1, -1, -1)
 
     def gather_steps(self):
         return [(CLIP, 2 * (1 << i)) for i in range(self.X.bit_length() - 1)] + [(CLIP, 1)]
@@ -242,18 +245,25 @@
             copy.wait_send()
 
 
+def flipped_bits(index, bits):
+    for b in range(bits.bit_length()):
+        if bits >> b & 1:
+            index = index + (1 << b) * (1 - 2 * ((index // (1 << b)) % 2))
+    return index
+
+
 def layer_kernel(plan, refs):
     D, T, S, L, FF, nj = plan.D, plan.T, plan.S, plan.L, plan.FF, plan.nj
     me = {CLIP: lax.axis_index(CLIP), FRAME: lax.axis_index(FRAME)}
     frame = me[FRAME]
     xin, gin, n1, qkv, prob, mixed = refs.xin, refs.gin, refs.n1, refs.qkv, refs.prob, refs.mixed
     mid, n2, act, slope, obuf, acc = refs.mid, refs.n2, refs.act, refs.slope, refs.obuf, refs.acc
-    dmid, sums = refs.dmid, refs.sums
+    sums = refs.sums
     for source, target in zip(refs.small, refs.small_rows):
         target[...] = source[...].reshape(1, -1)
     ln1_gain, ln1_bias, b_qv, b_out, ln2_gain, ln2_bias, b_up, b_down = refs.small_rows
     wqkv, wout, wup, wdown = refs.wqkv, refs.wout, refs.wup, refs.wdown
-    dbranch, dmixed, igbuf = n2, mixed, obuf
+    dbranch, dmixed, igbuf, dmid = n2, mixed, obuf, mid
 
     barrier = pltpu.get_barrier_semaphore()
     greeted = [(me[CLIP], lax.rem(frame + i, plan.F)) for i in range(1, plan.F)]
@@ -272,8 +282,8 @@
 
     def to_tubes(which, source, target, n):
         arriving = []
-        for i in range(plan.F):
-            peer = lax.rem(frame + i, plan.F)
+        for i in plan.peer_order():
+            peer = flipped_bits(frame, i)
             clip_set, positions = tubes(n, peer)
             src = source.at[:, clip_set, positions]
             dst = target.at[n, pl.ds(frame * plan.fd, plan.fd)]
@@ -298,8 +308,8 @@
 
     def to_frames(which, source, target, n):
         arriving = []
-        for i in range(plan.F):
-            peer = lax.rem(frame + i, plan.F)
+        for i in plan.peer_order():
+            peer = flipped_bits(frame, i)
             clip_set, positions = tubes(n, frame)
             src = source.at[n, pl.ds(peer * plan.fd, plan.fd)]
             dst = target.at[:, clip_set, positions]
@@ -383,9 +393,9 @@
             if part < len(scatters) and scatters[part].copies and not scatters[part].done():
                 scatters[part].advance()
 
-    def pieces(name, count, total, body):
+    def pieces(name, count, total, body, unroll=1):
         for i in range(count):
-            lax.fori_loop(total * i // count, total * (i + 1) // count, body, 0)
+            lax.fori_loop(total * i // count, total * (i + 1) // count, body, 0, unroll=unroll)
             tick(name + str(i))
 
     def seq_rows(ref, s, start, size):
@@ -400,6 +410,7 @@
 
     lanes = lax.broadcasted_iota(jnp.int32, (1, 128), 1)
     head_masks = [(lanes < 64).astype(BF16), (lanes >= 64).astype(BF16)]
+
     scale = 1.0 / math.sqrt(D // HEADS)
 
     def head_columns(pair):
@@ -445,7 +456,7 @@
             mixed[tokens, columns] = out.astype(BF16)
             return 0
 
-        lax.fori_loop(0, HEADS // 2, attend, 0)
+        lax.fori_loop(0, HEADS // 2, attend, 0, unroll=3)
 
     loads[1].wait()
 
@@ -527,12 +538,18 @@
         for f in range(plan.F):
             put(group, chunk, f, out[f * plan.R : (f + 1) * plan.R])
 
-    def grad_up(c, _):
+    core = lax.rem(me[CLIP], 2)
+
+    def grad_up(i, _):
+        c = lax.rem((1 - core) * plan.X + i, plan.C)
         grad_columns(1, c, n2[...], slope[:, ds(c * D, D)])
         return 0
 
-    pieces("GU", plan.C, plan.C, grad_up)
+    lax.fori_loop(0, plan.X, grad_up, 0)
+    tick("GU0")
     start(1)
+    lax.fori_loop(plan.X, plan.C, grad_up, 0)
+    tick("GU1")
     acc[...] = dot_nt(slope[...], wup[...])
     tick("DT")
 
@@ -585,14 +602,18 @@
             qkv[tokens, v_at] = d_v.astype(BF16)
             return 0
 
-        pieces("AB" + str(s), 2, HEADS // 2, attend_back)
-
-    def grad_qkv(c, _):
+        pieces("AB" + str(s), 2, HEADS // 2, attend_back, unroll=3)
+
+    def grad_qkv(i, _):
+        c = core * i + (1 - core) * lax.rem(plan.X + i + (i + 1) // plan.X, plan.C)
         grad_columns(2, c, n1[...], qkv[:, ds(c * D, D)])
         return 0
 
-    pieces("GQ", plan.C - 1, plan.C - 1, grad_qkv)
+    lax.fori_loop(0, plan.X, grad_qkv, 0)
+    tick("GQ0")
     start(2)
+    lax.fori_loop(plan.X, plan.C - 1, grad_qkv, 0)
+    tick("GQ1")
     acc[...] = dot_nt(qkv[...], wqkv[...])
     tick("D1")
     for recv, send in out_arrives:
@@ -684,7 +705,6 @@
         slope=vmem((T, FF)),
         obuf=vmem((S, FRAMES, plan.pos, D)),
         acc=vmem((T, D), F32),
-        dmid=vmem((T, D), F32),
         sums=vmem((n_vec, 8, D), F32),
         g_down=vmem((plan.whole, D)),
         g_up=vmem((plan.whole, D)),

time: 141 us -> 134 us (0.950)
  Pallas kernels: 139 us -> 133 us
    pallas_call x1, Pallas kernels: 135 us -> 128 us  [fused(): pl.pallas_call(kernel, out_shape=(jax.ShapeDtypeStruct(token_shape, BF16)...]
where the time goes in v3:
time: 134 us; the launch traced here: 133 us
  Pallas kernels  133 us (99%)
    pallas_call x1, Pallas kernels, fused(): pl.pallas_call(kernel, out_shape=(jax.ShapeDtypeStruct(token_shape, BF16)...  128 us
    pallas_call x1, Pallas kernels, finish(): pl.pallas_call(functools.partial(finish_kernel, plan), out_shape=tuple([l...  4.15 us

profile of v3, /device:TPU:1, one launch (start us, length us, event | category | flops | bytes accessed | tf_op | source)
XLA Modules:
  0.0 133.4 jit_solution(717227067820576038)
XLA Ops:
  0.7 128.4 %tube_layer.1 = (bf16[2,1,256,768]{3,2,1,0:T(8,128)(2,1)}, bf16[2,1,256,768]{3,2,1,0:T(8,128)(2,1)}, bf16[3,384,768]{2,1,0:T(8,128)(2,1)}, f32[24,768]{1,0:T(8,128)}) custom-call(bf16[2,1,256,768]{3,2,1,0:T(8,128)(2,1)} %bitcast.4, bf16[2,1,256,768]{3,2,1,0:T(8,128)(2,1)} %bitcast.5, bf16[768,2304]{1,0:T(8,128)(2,1)} %wqkv.1, bf16[768,768]{1,0:T(8,128)(2,1)} %wout.1, ...), custom_call_target="tpu_custom_call" | custom-call | tf_op jit(solution)/shard_map/tube_layer/pallas_call | solution.py:745
  129.0 4.2 %tube_layer_results.1 = (bf16[2,1,256,768]{3,2,1,0:T(8,128)(2,1)}, bf16[2,1,256,768]{3,2,1,0:T(8,128)(2,1)}, f32[96,2304]{1,0:T(8,128)}, f32[96,3072]{1,0:T(8,12...) custom-call(bf16[2,1,256,768]{3,2,1,0:T(8,128)(2,1)} %get-tuple-elem, ...), custom_call_target="tpu_custom_call" | custom-call | tf_op jit(solution)/shard_map/tube_layer_results/pallas_call | solution.py:844

commit v4 on v3

--- a/solution.py
+++ b/solution.py
@@ -772,13 +772,14 @@
 def finish_kernel(plan, out_s, ig_s, res_h, vec_h, out_d, ig_d, *refs):
     C, R, D = plan.C, plan.R, plan.D
     qkv_d, up_d, proj_d, down_d = refs[:4]
-    vectors, statistics = refs[4:12], refs[12]
-    qkv_v, up_v, proj_v, down_v, res, vec, out_v, ig_v, sems = refs[13:]
+    vectors_d, statistics_d = refs[4:12], refs[12]
+    qkv_v, up_v, proj_v, down_v, res, vec, out_v, ig_v = refs[13:21]
+    vectors, statistics, sems = refs[21:29], refs[29], refs[30]
     moves = [(res_h.at[group], res.at[group]) for group in range(3)]
     moves += [(vec_h, vec), (out_s, out_v), (ig_s, ig_v)]
     copies = [pltpu.make_async_copy(*move, sems.at[i]) for i, move in enumerate(moves)]
-    for copy in copies:
-        copy.start()
+    for i in (3, 0, 1, 2, 4, 5):
+        copies[i].start()
 
     def write(value, target):
         copy = pltpu.make_async_copy(value, target, sems.at[len(copies)])
@@ -791,6 +792,26 @@
                 for chunk in range(C):
                     block = res[group, pl.ds(first * C + chunk * height, height), :]
                     yield chunk, first, height, block.astype(F32)
+
+    copies[3].wait()
+    frame = lax.axis_index(FRAME)
+    counts = (1, 1, 2, 1, 1, 1, plan.nj, 1)
+    firsts = (0, 1, 2, 4, 5, 6, 13, 7)
+    for target, count, first in zip(vectors, counts, firsts):
+        share = count * D // plan.F
+        per_row = plan.F // count
+        row = vec[pl.ds(first + frame // per_row, 1), :]
+        turned = pltpu.roll(row, lax.rem(D - (frame % per_row) * share, D), 1)
+        target[...] = turned[:, :share].reshape(-1)
+    squares = jnp.sum(vec[pl.ds(8, 8), :], axis=-1, keepdims=True)
+    entries = plan.T * D * C * plan.F
+    roots = jnp.sqrt(squares / entries)
+    lanes = lax.broadcasted_iota(jnp.int32, (8, 8), 1)
+    rows = lax.broadcasted_iota(jnp.int32, (8, 8), 0)
+    across = jnp.sum(jnp.where(lanes == rows, roots, 0.0), axis=0, keepdims=True)
+    statistics[...] = across[:, :5].reshape(-1)
+    for value, target in zip((*vectors, statistics), (*vectors_d, statistics_d)):
+        write(value, target)
 
     copies[0].wait()
     for chunk, first, height, block in each_piece(0):
@@ -813,23 +834,6 @@
     copies[5].wait()
     write(ig_v, ig_d)
 
-    copies[3].wait()
-    frame = lax.axis_index(FRAME)
-    counts = (1, 1, 2, 1, 1, 1, plan.nj, 1)
-    firsts = (0, 1, 2, 4, 5, 6, 13, 7)
-    for target, count, first in zip(vectors, counts, firsts):
-        share = count * D // plan.F
-        per_row = plan.F // count
-        row = vec[pl.ds(first + frame // per_row, 1), :]
-        turned = pltpu.roll(row, lax.rem(D - (frame % per_row) * share, D), 1)
-        target[...] = turned[:, :share].reshape(-1)
-    squares = jnp.sum(vec[pl.ds(8, 8), :], axis=-1, keepdims=True)
-    entries = plan.T * D * C * plan.F
-    roots = jnp.sqrt(squares / entries)
-    lanes = lax.broadcasted_iota(jnp.int32, (8, 8), 1)
-    rows = lax.broadcasted_iota(jnp.int32, (8, 8), 0)
-    across = jnp.sum(jnp.where(lanes == rows, roots, 0.0), axis=0, keepdims=True)
-    statistics[...] = across[:, :5].reshape(-1)
     for copy in copies[6:]:
         copy.wait()
 
@@ -839,7 +843,6 @@
     shapes = [(R, 3 * D), (R, C * D), (R, D), (C * R, D)]
     vectors = [(count * D // F,) for count in (1, 1, 2, 1, 1, 1, plan.nj, 1)]
     hbm = pl.BlockSpec(memory_space=pltpu.HBM)
-    in_vmem = pl.BlockSpec(memory_space=pltpu.VMEM)
     like = lambda item: jax.ShapeDtypeStruct(item.shape, item.dtype)
     return pl.pallas_call(
         functools.partial(finish_kernel, plan),
@@ -848,11 +851,12 @@
             + [jax.ShapeDtypeStruct(shape, F32) for shape in shapes + vectors + [(5,)]]
         ),
         in_specs=[hbm] * 4,
-        out_specs=tuple([hbm] * 6 + [in_vmem] * 9),
+        out_specs=(hbm,) * 15,
         scratch_shapes=[pltpu.VMEM(shape, F32) for shape in shapes]
         + [pltpu.VMEM(res.shape, BF16), pltpu.VMEM(vec.shape, F32)]
         + [pltpu.VMEM(output.shape, BF16)] * 2
-        + [pltpu.SemaphoreType.DMA((12,))],
+        + [pltpu.VMEM(shape, F32) for shape in vectors + [(5,)]]
+        + [pltpu.SemaphoreType.DMA((21,))],
         compiler_params=pltpu.CompilerParams(vmem_limit_bytes=VMEM_LIMIT),
         name="tube_layer_results",
     )(output, input_grad, res, vec)

time: 134 us -> 133 us (level)
  no operation moved by 1% of the time
where the time goes in v4:
time: 133 us
  Pallas kernels  132 us (99%)
    pallas_call x1, Pallas kernels, fused(): pl.pallas_call(kernel, out_shape=(jax.ShapeDtypeStruct(token_shape, BF16)...  128 us
    pallas_call x1, Pallas kernels, finish(): pl.pallas_call(functools.partial(finish_kernel, plan), out_shape=tuple([l...  3.68 us

profile of v4, /device:TPU:1, one launch (start us, length us, event | category | flops | bytes accessed | tf_op | source)
XLA Modules:
  0.0 132.9 jit_solution(12376793257071696588)
XLA Ops:
  0.7 128.4 %tube_layer.1 = (bf16[2,1,256,768]{3,2,1,0:T(8,128)(2,1)}, bf16[2,1,256,768]{3,2,1,0:T(8,128)(2,1)}, bf16[3,384,768]{2,1,0:T(8,128)(2,1)}, f32[24,768]{1,0:T(8,128)}) custom-call(bf16[2,1,256,768]{3,2,1,0:T(8,128)(2,1)} %bitcast.4, bf16[2,1,256,768]{3,2,1,0:T(8,128)(2,1)} %bitcast.5, bf16[768,2304]{1,0:T(8,128)(2,1)} %wqkv.1, bf16[768,768]{1,0:T(8,128)(2,1)} %wout.1, ...), custom_call_target="tpu_custom_call" | custom-call | tf_op jit(solution)/shard_map/tube_layer/pallas_call | solution.py:745
  129.0 3.7 %tube_layer_results.1 = (bf16[2,1,256,768]{3,2,1,0:T(8,128)(2,1)}, bf16[2,1,256,768]{3,2,1,0:T(8,128)(2,1)}, f32[96,2304]{1,0:T(8,128)}, f32[96,3072]{1,0:T(8,12...) custom-call(bf16[2,1,256,768]{3,2,1,0:T(8,128)(2,1)} %get-tuple-elem, ...), custom_call_target="tpu_custom_call" | custom-call | tf_op jit(solution)/shard_map/tube_layer_results/pallas_call | solution.py:847

commit v5 on v4

--- a/solution.py
+++ b/solution.py
@@ -17,7 +17,7 @@
 F32 = jnp.float32
 BF16 = jnp.bfloat16
 MESH = pl.DeviceIdType.MESH
-ROW_BLOCK = 64
+ROW_BLOCK = 32
 CLIP = "clip"
 FRAME = "frame"
 

time: 133 us -> 140 us (1.053)
  Pallas kernels: 132 us -> 139 us
    pallas_call x1, Pallas kernels: 128 us -> 135 us  [fused(): pl.pallas_call(kernel, out_shape=(jax.ShapeDtypeStruct(token_shape, BF16)...]
where the time goes in v5:
time: 140 us
  Pallas kernels  139 us (99%)
    pallas_call x1, Pallas kernels, fused(): pl.pallas_call(kernel, out_shape=(jax.ShapeDtypeStruct(token_shape, BF16)...  135 us
    pallas_call x1, Pallas kernels, finish(): pl.pallas_call(functools.partial(finish_kernel, plan), out_shape=tuple([l...  3.68 us

profile of v5, /device:TPU:1, one launch (start us, length us, event | category | flops | bytes accessed | tf_op | source)
XLA Modules:
  0.0 139.8 jit_solution(2070502375245366479)
XLA Ops:
  0.7 135.2 %tube_layer.1 = (bf16[2,1,256,768]{3,2,1,0:T(8,128)(2,1)}, bf16[2,1,256,768]{3,2,1,0:T(8,128)(2,1)}, bf16[3,384,768]{2,1,0:T(8,128)(2,1)}, f32[24,768]{1,0:T(8,128)}) custom-call(bf16[2,1,256,768]{3,2,1,0:T(8,128)(2,1)} %bitcast.4, bf16[2,1,256,768]{3,2,1,0:T(8,128)(2,1)} %bitcast.5, bf16[768,2304]{1,0:T(8,128)(2,1)} %wqkv.1, bf16[768,768]{1,0:T(8,128)(2,1)} %wout.1, ...), custom_call_target="tpu_custom_call" | custom-call | tf_op jit(solution)/shard_map/tube_layer/pallas_call | solution.py:745
  135.9 3.7 %tube_layer_results.1 = (bf16[2,1,256,768]{3,2,1,0:T(8,128)(2,1)}, bf16[2,1,256,768]{3,2,1,0:T(8,128)(2,1)}, f32[96,2304]{1,0:T(8,128)}, f32[96,3072]{1,0:T(8,12...) custom-call(bf16[2,1,256,768]{3,2,1,0:T(8,128)(2,1)} %get-tuple-elem, ...), custom_call_target="tpu_custom_call" | custom-call | tf_op jit(solution)/shard_map/tube_layer_results/pallas_call | solution.py:847
